TPU v7x, 128 devices: a whole 4x4x4 slice. The times are simulated.
128 devices in a mesh: leaf: 64 (over z, x, y), grp: 2 (over core).
Axes of the slice: x: 4, y: 4, z: 4, core: 2. Of those that a mesh axis runs over, the one named last changes fastest.
Arguments:
- positions: float32 [3, 65536, 256], P(None, ('leaf', 'grp')), may hold values from 0 to 1
- charges: float32 [65536, 256], P(('leaf', 'grp')), may hold values from -0.12 to 0.12
- counts: int32 [65536], P(('leaf', 'grp')), may hold values from 96 to 256, as said below
- send_left: int32 [32768], P(('leaf', 'grp')), may hold values from 0 to 511, as said below
- pairs: int32 [3, 114688], P(None, ('leaf', 'grp')), may hold values from 0 to 767, as said below
Outputs:
- fields: float32 [4, 65536, 256], P(None, ('leaf', 'grp'))
Inputs may be any that keep to these rules, and one draw needn't show every extreme that they name: `counts`: each leaf holds at least 96 particles and in every device some leaf is full. `send_left`: within each device's 256 entries the indices are distinct. Each device's 896 columns are, in order: 512 self pairs (a, a, 13) of its leaves; 128 pairs of two different local leaves with a code other than 13; 256 pairs whose first leaf is a local leaf and whose second is 512 + k, naming the next device's k-th send_left leaf, with a code other than 13.
All inputs are finite; a program needn't handle non-finite values.
Results may differ from a plain program's by a relative error of at most 0.0003.
Values sent between devices are 32-bit elements; how exact they have to be, the bound alone decides.
A program may use at most 64 MiB of HBM per device.

v0:
```python
import jax
import jax.numpy as jnp
from jax import lax
from jax.sharding import PartitionSpec as P

SOFTEN = 0.05


def shifted(value, axis, by):
    length = lax.axis_size(axis)
    pairs = [(i, i + by) for i in range(length) if 0 <= i + by < length]
    return lax.ppermute(value, axis, pairs)


def offsets(code):
    return jnp.stack([code // 9 - 1, code // 3 % 3 - 1, code % 3 - 1]).astype(jnp.float32)


def pair_terms(target, source, displace, coincide, first_slot):
    slots_t = target.shape[2]
    slots_s = source.shape[2]
    diff = target[:3, :, :, None] - (source[:3, :, None, :] + displace[:, :, None, None])
    radius2 = jnp.sum(diff * diff, axis=0) + SOFTEN
    diagonal = (jnp.arange(slots_t)[:, None] + first_slot == jnp.arange(slots_s)[None, :]).astype(
        jnp.float32
    )
    weight = 1.0 / jnp.sqrt(radius2) * (1.0 - coincide[:, None, None] * diagonal[None])
    cubed = weight * weight * weight
    charge_s = source[3][:, None, :]
    charge_t = target[3][:, :, None]
    phi_t = jnp.sum(weight * charge_s, axis=2)
    field_t = jnp.sum(diff * (cubed * charge_s)[None], axis=3)
    phi_s = jnp.sum(weight * charge_t, axis=1)
    field_s = -jnp.sum(diff * (cubed * charge_t)[None], axis=2)
    return (jnp.concatenate([phi_t[None], field_t], 0), jnp.concatenate([phi_s[None], field_s], 0))


def block_terms(target, source, displace, coincide):
    quarter_len = target.shape[2] // 4
    target_parts = []
    source_total = jnp.zeros(source.shape, jnp.float32)
    for quarter in range(4):
        first_slot = quarter * quarter_len
        piece = target[:, :, first_slot : first_slot + quarter_len]
        on_target, on_source = pair_terms(piece, source, displace, coincide, first_slot)
        target_parts.append(on_target)
        source_total = source_total + on_source
    return (jnp.concatenate(target_parts, 2), source_total)


def accumulate(pool, pair_rows, local_leaves):
    block = local_leaves // 16
    blocks = pair_rows.shape[1] // block
    rows = pair_rows.reshape(3, blocks, block)

    def step(totals, inputs):
        first_leaf, second_leaf, kind = inputs
        target = jnp.take(pool, first_leaf, axis=1)
        source = jnp.take(pool, second_leaf, axis=1)
        coincide = (first_leaf == second_leaf).astype(jnp.float32)
        on_target, on_source = block_terms(target, source, offsets(kind), coincide)
        totals = totals.at[:, first_leaf].add(on_target)
        keep = 1.0 - coincide
        totals = totals.at[:, second_leaf].add(on_source * keep[None, :, None])
        return (totals, None)

    totals, unused = lax.scan(step, jnp.zeros(pool.shape, jnp.float32), (rows[0], rows[1], rows[2]))
    return totals


def on_device(positions, charges, counts, send_left, pairs):
    local_leaves = positions.shape[1]
    slots = positions.shape[2]
    occupied = (jnp.arange(slots)[None, :] < counts[:, None]).astype(jnp.float32)
    sources = jnp.concatenate([positions, (charges * occupied)[None]], 0)
    outgoing = jnp.take(sources, send_left, axis=1)
    remote = shifted(outgoing, ("leaf", "grp"), -1)
    pool = jnp.concatenate([sources, remote], 1)
    totals = accumulate(pool, pairs, local_leaves)
    returned = shifted(totals[:, local_leaves:], ("leaf", "grp"), 1)
    own = totals[:, :local_leaves].at[:, send_left].add(returned)
    return own * occupied[None]


def solution(mesh):
    in_specs = (
        P(None, ("leaf", "grp"), None),
        P(("leaf", "grp"), None),
        P(("leaf", "grp")),
        P(("leaf", "grp")),
        P(None, ("leaf", "grp")),
    )
    out_specs = P(None, ("leaf", "grp"), None)
    return jax.shard_map(
        on_device, mesh=mesh, in_specs=in_specs, out_specs=out_specs, check_vma=False
    )
```

profile of v0, /device:TPU:96, one launch (start us, length us, event | category | flops | bytes accessed | tf_op | source)
XLA Modules:
  0.0 997.6 jit_solution(1797880678791956266)
XLA Ops:
  13.1 6.6 collective-permute-start
  20.5 11.6 %collective-permute-done = f32[4,256,256]{2,0,1:T(4,128)} collective-permute-done((f32[4,256,256]{2,0,1:T(4,128)}, f32[4,256,256]{2,0,1:T(4,128)}, u32[]{:S(2)}, u32[]{:S(2)}) %collective-permute-start) | collective-permute-done | bytes 1048608 | tf_op jit(solution)/shard_map/ppermute | solution.py:12
  36.5 906.1 %while.13 = (s32[]{:T(128)}, f32[4,768,256]{2,0,1:T(4,128)S(1)}, s32[28,32]{1,0:T(8,128)S(1)}, f32[4,768,256]{2,0,1:T(4,128)}, s32[28,32]{1,0:T(8,128)S(1)}, /*index=5*/s32[28,32]{1,0:T(8,128)}, s32[]{:T(128)}) while((s32[]{:T(128)}, f32[4,768,256]{2,0,1:T(4,128)S(1)}, s32[28,32]{1,0:T(8,128)S(1)}, f32[4,768,256]{2,0,1:T(4,128)}, ...), condition=%wide.region_23.25_spmd, body=%wide.region_0.24_spmd.sunk | while | flops 78311392 | bytes 61504220 | solution.py:67
  47.1 7.3 fusion.55
  59.2 5.8 fusion.57
  79.4 7.3 fusion.55
  91.6 5.8 fusion.57
  111.8 7.3 fusion.55
  123.9 5.8 fusion.57
  144.2 7.3 fusion.55
  156.3 5.8 fusion.57
  176.5 7.3 fusion.55
  183.9 4.7 multiply_reduce_fusion.9
  188.7 5.8 fusion.57
  208.9 7.3 fusion.55
  221.0 5.8 fusion.57
  241.3 7.3 fusion.55
  253.4 5.8 fusion.57
  273.6 7.3 fusion.55
  285.8 5.8 fusion.57
  306.0 7.3 fusion.55
  318.1 5.8 fusion.57
  338.3 7.3 fusion.55
  350.5 5.8 fusion.57
  370.7 7.3 fusion.55
  382.8 5.8 fusion.57
  403.1 7.3 fusion.55
  410.4 4.7 multiply_reduce_fusion.9
  415.2 5.8 fusion.57
  435.4 7.3 fusion.55
  447.5 5.8 fusion.57
  467.8 7.3 fusion.55
  479.9 5.8 fusion.57
  500.1 7.3 fusion.55
  507.5 4.7 multiply_reduce_fusion.9
  512.3 5.8 fusion.57
  532.5 7.3 fusion.55
  544.6 5.8 fusion.57
  564.8 7.3 fusion.55
  577.0 5.8 fusion.57
  597.2 7.3 fusion.55
  609.3 5.8 fusion.57
  629.6 7.3 fusion.55
  641.7 5.8 fusion.57
  661.9 7.3 fusion.55
  674.0 5.8 fusion.57
  694.3 7.3 fusion.55
  706.4 5.8 fusion.57
  726.6 7.3 fusion.55
  738.8 5.8 fusion.57
  759.0 7.3 fusion.55
  771.1 5.8 fusion.57
  791.3 7.3 fusion.55
  803.5 5.8 fusion.57
  823.7 7.3 fusion.55
  835.8 5.8 fusion.57
  856.1 7.3 fusion.55
  868.2 5.8 fusion.57
  888.4 7.3 fusion.55
  900.5 5.8 fusion.57
  920.8 7.3 fusion.55
  932.9 5.8 fusion.57
  947.4 16.0 %collective-permute-done.1 = f32[4,256,256]{2,0,1:T(4,128)} collective-permute-done((f32[4,256,256]{2,0,1:T(4,128)S(1)}, f32[4,256,256]{2,0,1:T(4,128)}, u32[]{:S(2)}, u32[]{:S(2)}) %collective-permute-start.1) | collective-permute-done | bytes 1048608 | tf_op jit(solution)/shard_map/ppermute | solution.py:12
  963.4 30.4 %scatter_fusion.2 = f32[4,512,256]{2,0,1:T(4,128)} fusion(f32[4,512,256]{2,0,1:T(4,128)} %slice.109, s32[256]{0:T(256)S(1)} %compare_select_fusion.4, f32[256,4,256]{2,1,0:T(4,128)} %bitcast.23), kind=kCustom, calls=%fused_computation.5 | custom fusion | flops 262144 | bytes 3146752 | tf_op jit(solution)/shard_map/scatter-add | solution.py:81
  (1148 shorter events, 544.7 us)
Async XLA Ops:
  0.0 3.9 copy-start.1
  0.0 3.9 copy-start.2
  6.7 12.9 %copy-start.4 = (s32[3,896]{1,0:T(4,128)S(1)}, s32[3,896]{1,0:T(4,128)}, u32[]{:S(2)}) copy-start(s32[3,896]{1,0:T(4,128)} %param.13) | copy-start | bytes 32260
  13.1 19.0 %collective-permute-start = (f32[4,256,256]{2,0,1:T(4,128)}, f32[4,256,256]{2,0,1:T(4,128)}, u32[]{:S(2)}, u32[]{:S(2)}) collective-permute-start(f32[4,256,256]{2,0,1:T(4,128)} %select_bitcast_fusion.2), channel_id=1, source_target_pairs={{1,0},{2,1},{3,2},{4,3},{5,4},{6,5},{7,6},{8,7},{9,8},{10,9},{11,1... | collective-permute-start | bytes 3145736 | tf_op jit(solution)/shard_map/ppermute | solution.py:12
  942.6 2.1 copy-start.3
  942.8 20.6 %collective-permute-start.1 = (f32[4,256,256]{2,0,1:T(4,128)S(1)}, f32[4,256,256]{2,0,1:T(4,128)}, u32[]{:S(2)}, u32[]{:S(2)}) collective-permute-start(f32[4,256,256]{2,0,1:T(4,128)S(1)} %slice.110), channel_id=1, source_target_pairs={{0,1},{1,2},{2,3},{3,4},{4,5},{5,6},{6,7},{7,8},{8,9},{9,10},{10,1... | collective-permute-start | bytes 3145736 | tf_op jit(solution)/shard_map/ppermute | solution.py:12
  947.4 46.4 %copy-start = (f32[512,256]{1,0:T(8,128)S(1)}, f32[512,256]{1,0:T(8,128)}, u32[]{:S(2)}) copy-start(f32[512,256]{1,0:T(8,128)} %fusion.33) | copy-start | bytes 1572868
where the time goes:
time: 1000 us; the launch traced here: 998 us
  other arithmetic  783 us (78%)
  local copies, waits for them, and re-layouts  170 us (17%)
  waiting for transfers between devices  27.6 us (3%)
    reduce_sum x56, other arithmetic, pair_terms(): field_s = -jnp.sum(diff * (cubed * charge_t)[None], axis=2)  366 us
    reduce_sum x28, other arithmetic, pair_terms(): phi_s = jnp.sum(weight * charge_t, axis=1)  133 us
    gather x28, local copies, waits for them, and re-layouts, step(): target = jnp.take(pool, first_leaf, axis=1)  70.6 us
    gather x28, local copies, waits for them, and re-layouts, step(): source = jnp.take(pool, second_leaf, axis=1)  70.6 us
    reduce_sum x28, other arithmetic, pair_terms(): radius2 = jnp.sum(diff * diff, axis=0) + SOFTEN  64 us
    scatter-add x28, other arithmetic, step(): totals = totals.at[:, second_leaf].add(on_source * keep[None, :, None])  47.4 us
    scatter-add x28, other arithmetic, step(): totals = totals.at[:, first_leaf].add(on_target)  47.4 us
    mul x28, other arithmetic, pair_terms(): field_t = jnp.sum(diff * (cubed * charge_s)[None], axis=3)  40.2 us
  transfers between devices with their start and end apart: 2, of which 2 were waited for; matrix products, arithmetic and copies ran while one was open for 0% of the time, Pallas kernels for 0%

commit v1 on v0

v1 whole, which is shorter than its diff:
```python
import functools
import numpy as np
import jax, jax.numpy as jnp
from jax import lax
from jax.experimental import pallas as pl
from jax.experimental.pallas import tpu as pltpu
from jax.sharding import PartitionSpec as P

F32 = jnp.float32
BF16 = jnp.bfloat16
SOFTEN = 0.05
CELL = 128
NN = (((1,), (0,)), ((), ()))
TN = (((0,), (0,)), ((), ()))


def offset_tables():
    code = np.arange(27)
    o = np.stack([code // 9 - 1, code // 3 % 3 - 1, code % 3 - 1], 1).astype(np.float32)
    scale = np.zeros((27, 16), np.float32)
    scale[:, 0:3] = 2 * o
    scale[:, 8:11] = 2 * o
    const = np.zeros((27, 16), np.float32)
    const[:, 3] = (o * o).sum(1)
    const[:, 4:7] = o
    const[:, 7] = 1
    const[:, 11] = 1
    const[:, 12:15] = o
    shift = np.zeros((27, 16), np.float32)
    shift[:, 0:3] = o
    shift[:, 4:7] = o * o
    shift[:, 12:15] = 2 * o
    wide = lambda t: np.broadcast_to(t[:, :, None], (27, 16, CELL))
    return jnp.asarray(wide(scale), BF16), jnp.asarray(wide(const), BF16), jnp.asarray(wide(shift), F32)


def rounded(x):
    return x.astype(BF16).astype(F32)


def two_parts(x):
    high = rounded(x)
    return high, rounded(x - high)


def three_parts(x):
    high, middle = two_parts(x)
    return high, middle, x - high - middle


def features(pos, q, rows_r, rows_q, rows_l):
    highs, mids, coords = [], [], []
    for x in pos:
        high, mid = two_parts(x - 0.5)
        highs.append(high)
        mids.append(mid)
        coords.append(high + mid)
    squares = [c * c for c in coords]
    norm = squares[0] + squares[1] + squares[2]
    s = three_parts(norm)
    for i in range(3):
        for base in (0, 4):
            rows_r[pl.ds(base + i, 8, stride=16), :] = highs[i]
            rows_r[pl.ds(8 + base + i, 8, stride=16), :] = mids[i]
    one = jnp.ones_like(q)
    rows_r[pl.ds(3, 8, stride=16), :] = one
    rows_r[pl.ds(7, 8, stride=16), :] = s[0]
    rows_r[pl.ds(11, 8, stride=16), :] = s[2]
    rows_r[pl.ds(15, 8, stride=16), :] = s[1]
    for i in range(3):
        for row, value in ((i, coords[i]), (4 + i, squares[i])):
            high, mid = two_parts(q * value)
            rows_q[pl.ds(row, 8, stride=16), :] = high
            rows_q[pl.ds(8 + row, 8, stride=16), :] = mid
    high, mid = two_parts(q)
    rows_q[pl.ds(3, 8, stride=16), :] = high
    rows_q[pl.ds(11, 8, stride=16), :] = mid
    if rows_l is not None:
        n = three_parts(norm + SOFTEN)
        for i in range(3):
            h, m = -2.0 * highs[i], -2.0 * mids[i]
            rows_l[pl.ds(i, 8, stride=32), :] = h
            rows_l[pl.ds(4 + i, 8, stride=32), :] = m
            rows_l[pl.ds(8 + i, 8, stride=32), :] = h
            rows_l[pl.ds(12 + i, 8, stride=32), :] = m
            rows_l[pl.ds(20 + i, 8, stride=32), :] = h
            rows_l[pl.ds(28 + i, 8, stride=32), :] = m
        rows_l[pl.ds(3, 8, stride=32), :] = n[0]
        rows_l[pl.ds(23, 8, stride=32), :] = n[1]
        rows_l[pl.ds(27, 8, stride=32), :] = n[2]


def prepare(pos_at, q_at, leaves, slots, stage_r, stage_q, stage_l, R, Q, L):
    halves = slots // CELL
    for h in range(halves):
        stage_q[h, pl.ds(7, 8, stride=16), :] = jnp.zeros((8, CELL), F32)
        stage_q[h, pl.ds(15, 8, stride=16), :] = jnp.zeros((8, CELL), F32)
        if L is not None:
            for row in (7, 11, 15, 16, 17, 18, 19, 24, 25, 26):
                stage_l[h, pl.ds(row, 8, stride=32), :] = jnp.ones((8, CELL), F32)
            stage_l[h, pl.ds(31, 8, stride=32), :] = jnp.zeros((8, CELL), F32)

    @pl.loop(0, leaves // 8)
    def _(g):
        first = pl.multiple_of(g * 8, 8)
        for h in range(halves):
            lanes = slice(h * CELL, (h + 1) * CELL)
            pos = [pos_at(i, pl.ds(first, 8), lanes) for i in range(3)]
            q = q_at(pl.ds(first, 8), lanes)
            features(pos, q, stage_r.at[h], stage_q.at[h], None if L is None else stage_l.at[h])
            to = pl.ds(h * leaves + first, 8)
            R[to] = stage_r[h].reshape(8, 16, CELL).astype(BF16)
            Q[to] = stage_q[h].reshape(8, 16, CELL).astype(BF16)
            if L is not None:
                L[to] = stage_l[h].reshape(8, 32, CELL).astype(BF16)


def cell_loop(U, items, batches, scale, const, shift, L, Qa, acc_a, R, Qb, acc_b, gram, weights, turned, both):
    def decode(i):
        e = items[i]
        return e & 2047, (e >> 11) & 2047, e >> 22

    def add(acc, at, q, w, code):
        out = lax.dot_general(jnp.concatenate([q, q], 1), w, NN, preferred_element_type=F32)
        m = out[0:8] + out[8:16]
        if both:
            a = jnp.broadcast_to(m[3:4], m.shape)
            m = m + shift[code, 0:8] * a + shift[code, 8:16] * pltpu.roll(m, 4, 0)
        acc[at] += m

    @pl.loop(0, batches + 3)
    def _(j):
        if both:
            for k in range(U):
                a, b, code = decode(j * U + k)
                add(acc_a, a, Qb[b], turned[k], code)
        for k in range(U):
            a, b, code = decode((j + 1) * U + k)
            w = weights[k]
            if both:
                add(acc_b, b, Qa[a], w, 26 - code)
                turned[k, 0:CELL] = w[0:CELL].T
                turned[k, CELL:] = w[CELL:].T
            else:
                add(acc_a, a, Qb[b], w, code)
        for k in range(U):
            w = lax.rsqrt(gram[k])
            w3 = w * w * w
            high = w3.astype(BF16)
            weights[k, 0:CELL] = high
            weights[k, CELL:] = (w3 - high.astype(F32)).astype(BF16)
        for k in range(U):
            a, b, code = decode((j + 3) * U + k)
            r0 = R[b]
            r1 = r0 * scale[code] + const[code]
            gram[k] = lax.dot_general(L[a], jnp.concatenate([r0, r1], 0), TN, preferred_element_type=F32)


def batches_of(n, U):
    return lax.div(n + U - 1, U)


def idle(dummy_a, dummy_b):
    return dummy_a + dummy_b * 2048 + 13 * (1 << 22)


def fill(items, start, n, value):
    @pl.loop(0, n)
    def _(i):
        items[start + i] = value


def local_kernel(U, leaves, slots, npairs, pos, q, counts, pairs, scale, const, shift, acc, L, Q, R, stage_r, stage_q,
                 stage_l, diag, cross, gram, weights, turned):
    dummy = 2 * leaves
    acc[...] = jnp.zeros_like(acc)
    R[dummy] = jnp.zeros(R.shape[1:], BF16)
    Q[dummy] = jnp.zeros(Q.shape[1:], BF16)
    L[dummy] = jnp.ones(L.shape[1:], BF16)
    gram[...] = jnp.ones_like(gram)
    weights[...] = jnp.zeros_like(weights)
    turned[...] = jnp.zeros_like(turned)
    none = idle(dummy, dummy)
    for k in range(3 * U):
        diag[k] = none
        cross[k] = none
    prepare(lambda i, r, s: pos[i, r, s], lambda r, s: q[r, s], leaves, slots, stage_r, stage_q, stage_l, R, Q, L)
    code0 = 13 * (1 << 22)

    def own(l, carry):
        nd, nx = carry
        more = (counts[l] > CELL).astype(jnp.int32)
        diag[nd] = l * 2049 + code0
        diag[nd + 1] = (l + leaves) * 2049 + code0
        cross[nx] = l + (l + leaves) * 2048 + code0
        return nd + 1 + more, nx + more

    nd, nx = lax.fori_loop(0, leaves, own, (3 * U, 3 * U), unroll=8)

    def near(i, nx):
        a, b, code = pairs[0, i], pairs[1, i], pairs[2, i]
        more_a = (counts[a] > CELL).astype(jnp.int32)
        more_b = (counts[b] > CELL).astype(jnp.int32)
        e = a + b * 2048 + code * (1 << 22)
        cross[nx] = e
        nx += 1
        cross[nx] = e + leaves
        nx += more_a
        cross[nx] = e + leaves * 2048
        nx += more_b
        cross[nx] = e + leaves * 2049
        return nx + more_a * more_b

    nx = lax.fori_loop(leaves, leaves + npairs, near, nx, unroll=4)
    fill(diag, nd, 5 * U, none)
    fill(cross, nx, 5 * U, none)
    loop = functools.partial(cell_loop, U)
    loop(diag, batches_of(nd - 3 * U, U), scale, const, shift, L, Q, acc, R, Q, acc, gram, weights, turned, False)
    weights[...] = jnp.zeros_like(weights)
    loop(cross, batches_of(nx - 3 * U, U), scale, const, shift, L, Q, acc, R, Q, acc, gram, weights, turned, True)


def remote_kernel(U, leaves, remotes, slots, npairs, first, rpos, counts, rcounts, pairs, scale, const, shift, L, Qa,
                  acc_in, acc, back, R, Q, acc_b, stage_r, stage_q, cross, gram, weights, turned):
    dummy_a, dummy_b = 2 * leaves, 2 * remotes
    acc[...] = acc_in[...]
    acc_b[...] = jnp.zeros_like(acc_b)
    R[dummy_b] = jnp.zeros(R.shape[1:], BF16)
    Q[dummy_b] = jnp.zeros(Q.shape[1:], BF16)
    gram[...] = jnp.ones_like(gram)
    weights[...] = jnp.zeros_like(weights)
    turned[...] = jnp.zeros_like(turned)
    none = idle(dummy_a, dummy_b)
    for k in range(3 * U):
        cross[k] = none
    prepare(lambda i, r, s: rpos[i, r, s], lambda r, s: rpos[3, r, s], remotes, slots, stage_r, stage_q, None, R, Q, None)

    def far(i, nx):
        a, b, code = pairs[0, i], pairs[1, i] - leaves, pairs[2, i]
        more_a = (counts[a] > CELL).astype(jnp.int32)
        more_b = (rcounts[b] > CELL).astype(jnp.int32)
        e = a + b * 2048 + code * (1 << 22)
        cross[nx] = e
        nx += 1
        cross[nx] = e + leaves
        nx += more_a
        cross[nx] = e + remotes * 2048
        nx += more_b
        cross[nx] = e + remotes * 2048 + leaves
        return nx + more_a * more_b

    nx = lax.fori_loop(first, first + npairs, far, 3 * U, unroll=4)
    fill(cross, nx, 5 * U, none)
    cell_loop(U, cross, batches_of(nx - 3 * U, U), scale, const, shift, L, Qa, acc, R, Q, acc_b, gram, weights, turned, True)

    @pl.loop(0, remotes // 8)
    def _(g):
        r = pl.ds(pl.multiple_of(g * 8, 8), 8)
        for h in range(slots // CELL):
            lanes = slice(h * CELL, (h + 1) * CELL)
            cells = pl.ds(pl.multiple_of(h * remotes + g * 8, 8), 8)
            values = finished(acc_b, cells, [rpos[i, r, lanes] for i in range(3)])
            for i in range(4):
                back[i, r, lanes] = values[i]


def finished(acc, cells, pos):
    u = [sum(two_parts(x - 0.5)) for x in pos]
    total = acc[cells, 3, :]
    moments = [acc[cells, i, :] for i in range(3)]
    square = acc[cells, 4, :] + acc[cells, 5, :] + acc[cells, 6, :]
    norm = u[0] * u[0] + u[1] * u[1] + u[2] * u[2]
    dots = u[0] * moments[0] + u[1] * moments[1] + u[2] * moments[2]
    phi = (norm + SOFTEN) * total - 2.0 * dots + square
    return [phi] + [u[i] * total - moments[i] for i in range(3)]


def final_kernel(leaves, remotes, slots, acc, pos, q, occupied, send, back, out):
    @pl.loop(0, leaves // 8)
    def _(g):
        r = pl.ds(pl.multiple_of(g * 8, 8), 8)
        for h in range(slots // CELL):
            lanes = slice(h * CELL, (h + 1) * CELL)
            cells = pl.ds(pl.multiple_of(h * leaves + g * 8, 8), 8)
            values = finished(acc, cells, [pos[i, r, lanes] for i in range(3)])
            values[0] = values[0] - q[r, lanes] * (1.0 / np.sqrt(SOFTEN))
            for i in range(4):
                out[i, r, lanes] = values[i]

    if send is not None:
        def give(k, _):
            l = send[k]
            for i in range(4):
                out[i, pl.ds(l, 1), :] += back[i, pl.ds(k, 1), :]
            return 0
        lax.fori_loop(0, remotes, give, 0, unroll=8)

    @pl.loop(0, leaves // 8)
    def _(g):
        r = pl.ds(pl.multiple_of(g * 8, 8), 8)
        for i in range(4):
            out[i, r, :] = out[i, r, :] * occupied[r, :]


SMEM = pl.BlockSpec(memory_space=pltpu.SMEM)
VMEM = pl.BlockSpec(memory_space=pltpu.VMEM)
PARAMS = pltpu.CompilerParams(vmem_limit_bytes=58 << 20)


def scratch_loop(U):
    return [pltpu.VMEM((U, CELL, CELL), F32)] + [pltpu.VMEM((U, 2 * CELL, CELL), BF16)] * 2


def local_call(U, pos, q, counts, pairs, tables, npairs):
    leaves, slots = q.shape
    cells = 2 * leaves + 1
    return pl.pallas_call(
        functools.partial(local_kernel, U, leaves, slots, npairs),
        out_shape=(jax.ShapeDtypeStruct((cells, 8, CELL), F32), jax.ShapeDtypeStruct((cells, 32, CELL), BF16),
                   jax.ShapeDtypeStruct((cells, 16, CELL), BF16)),
        in_specs=[VMEM, VMEM, SMEM, SMEM, VMEM, VMEM, VMEM],
        out_specs=(VMEM, VMEM, VMEM),
        scratch_shapes=[pltpu.VMEM((cells, 16, CELL), BF16), pltpu.VMEM((2, 128, CELL), F32),
                        pltpu.VMEM((2, 128, CELL), F32), pltpu.VMEM((2, 256, CELL), F32),
                        pltpu.SMEM((2 * leaves + 9 * U,), jnp.int32),
                        pltpu.SMEM((leaves + 4 * npairs + 9 * U + 4,), jnp.int32)] + scratch_loop(U),
        compiler_params=PARAMS, name="local")(pos, q, counts, pairs, *tables)


def remote_call(U, rpos, counts, rcounts, pairs, tables, L, Q, acc, first, npairs):
    leaves = counts.shape[0]
    remotes, slots = rpos.shape[1:]
    cells = 2 * remotes + 1
    return pl.pallas_call(
        functools.partial(remote_kernel, U, leaves, remotes, slots, npairs, first),
        out_shape=(jax.ShapeDtypeStruct(acc.shape, F32), jax.ShapeDtypeStruct(rpos.shape, F32)),
        in_specs=[VMEM, SMEM, SMEM, SMEM, VMEM, VMEM, VMEM, VMEM, VMEM, VMEM],
        out_specs=(VMEM, VMEM),
        scratch_shapes=[pltpu.VMEM((cells, 16, CELL), BF16), pltpu.VMEM((cells, 16, CELL), BF16),
                        pltpu.VMEM((cells, 8, CELL), F32), pltpu.VMEM((2, 128, CELL), F32),
                        pltpu.VMEM((2, 128, CELL), F32),
                        pltpu.SMEM((4 * npairs + 9 * U + 4,), jnp.int32)] + scratch_loop(U),
        compiler_params=PARAMS, name="remote")(rpos, counts, rcounts, pairs, *tables, L, Q, acc)


def final_call(acc, pos, q, occupied, send, back):
    leaves, slots = q.shape
    remotes = back.shape[1]
    return pl.pallas_call(
        functools.partial(final_kernel, leaves, remotes, slots),
        out_shape=jax.ShapeDtypeStruct((4, leaves, slots), F32),
        in_specs=[VMEM, VMEM, VMEM, VMEM, SMEM, VMEM], out_specs=VMEM,
        compiler_params=PARAMS, name="final")(acc, pos, q, occupied, send, back)


def shifted(value, axis, by):
    length = lax.axis_size(axis)
    return lax.ppermute(value, axis, [(i, i + by) for i in range(length) if 0 <= i + by < length])


AXES = ("leaf", "grp")
GROUP = 16


def on_device(positions, charges, counts, send_left, pairs):
    leaves, slots = charges.shape
    remotes = send_left.shape[0]
    near = pairs.shape[1] - leaves - remotes
    occupied = (jnp.arange(slots)[None, :] < counts[:, None]).astype(jnp.float32)
    charges = charges * occupied
    tables = offset_tables()
    outgoing = jnp.take(jnp.concatenate([positions, charges[None]], 0), send_left, axis=1)
    remote = shifted(outgoing, AXES, -1)
    remote_counts = shifted(jnp.take(counts, send_left), AXES, -1)
    acc, L, Q = local_call(GROUP, positions, charges, counts, pairs, tables, near)
    acc, back = remote_call(GROUP, remote, counts, remote_counts, pairs, tables, L, Q, acc, leaves + near, remotes)
    returned = shifted(back, AXES, 1)
    return final_call(acc, positions, charges, occupied, send_left, returned)


def solution(mesh):
    in_specs = (P(None, AXES, None), P(AXES, None), P(AXES), P(AXES), P(None, AXES))
    return jax.shard_map(on_device, mesh=mesh, in_specs=in_specs, out_specs=P(None, AXES, None), check_vma=False)
```

time: 1000 us -> 208 us (0.21)
  other arithmetic: 783 us -> 4.74 us
  Pallas kernels: 0 us -> 166 us
  local copies, waits for them, and re-layouts: 170 us -> 9.07 us
  waiting for transfers between devices: 27.6 us -> 17.6 us
    reduce_sum x112 -> x0, other arithmetic: 563 us -> none  [the longest x56 366 us: pair_terms(): field_s = -jnp.sum(diff * (cubed * charge_t)[None], axis=2)]
    pallas_call x0 -> x3, Pallas kernels: none -> 166 us  [the longest x1 97.7 us: local_call(): pl.pallas_call(functools.partial(local_kernel, U, leaves, slots, npairs),...]
    gather x57 -> x2, local copies, waits for them, and re-layouts: 145 us -> 3.26 us  [the longest x1 1.99 us: on_device(): remote_counts = shifted(jnp.take(counts, send_left), AXES, -1)]
    scatter-add x57 -> x0, other arithmetic: 125 us -> none  [the longest x28 47.4 us: step(): totals = totals.at[:, second_leaf].add(on_source * keep[None, :, None])]
    mul x58 -> x1, other arithmetic: 44.8 us -> 0.97 us  [on_device(): charges = charges * occupied]
    sub x56 -> x0, other arithmetic: 20.4 us -> none  [the longest x28 19.9 us: offsets(): code // 9 - 1]
    slice x199 -> x0, local copies, waits for them, and re-layouts: 11 us -> none  [the longest x140 4.2 us: pair_terms(): target[:3, :, :, None]]
    ppermute x2 -> x3, waiting for transfers between devices: 27.6 us -> 17.6 us  [shifted(): lax.ppermute(value, axis, [(i, i + by) for i in range(length) if 0 <= i +...]
  transfers between devices with their start and end apart: 2 -> 3, of which waited for: 2 -> 1; matrix products, arithmetic and copies ran while one was open for 0% -> 1% of each run, Pallas kernels for 0% -> 47%
where the time goes in v1:
time: 208 us
  Pallas kernels  166 us (80%)
  waiting for transfers between devices  17.6 us (8%)
  starting transfers between devices  10.9 us (5%)
  local copies, waits for them, and re-layouts  9.07 us (4%)
  other arithmetic  4.74 us (2%)
    pallas_call x1, Pallas kernels, local_call(): pl.pallas_call(functools.partial(local_kernel, U, leaves, slots, npairs),...  97.7 us
    pallas_call x1, Pallas kernels, remote_call(): pl.pallas_call(functools.partial(remote_kernel, U, leaves, remotes, slots...  58.5 us
    ppermute x3, waiting for transfers between devices, shifted(): lax.ppermute(value, axis, [(i, i + by) for i in range(length) if 0 <= i +...  17.6 us
    ppermute x3, starting transfers between devices, shifted(): lax.ppermute(value, axis, [(i, i + by) for i in range(length) if 0 <= i +...  10.9 us
    pallas_call x1, Pallas kernels, final_call(): pl.pallas_call(functools.partial(final_kernel, leaves, remotes, slots), o...  9.32 us
    unnamed x17, local copies, waits for them, and re-layouts  4.45 us
  transfers between devices with their start and end apart: 3, of which 1 were waited for; matrix products, arithmetic and copies ran while one was open for 1% of the time, Pallas kernels for 47%

profile of v1, /device:TPU:96, one launch (start us, length us, event | category | flops | bytes accessed | tf_op | source)
XLA Modules:
  0.0 208.0 jit_solution(15083738153246502426)
XLA Ops:
  0.0 0.7 compare_select_fusion
  0.7 2.0 gather_fusion.1
  2.7 0.0 copy-start
  2.7 0.0 copy-start.2
  2.7 0.7 broadcast_select_fusion
  3.4 2.5 %copy.9 = f32[3,512,256]{2,0,1:T(4,128)S(1)} copy(f32[3,512,256]{2,1,0:T(8,128)} %pos.3) | data formatting | bytes 3145728 | tf_op args[0]
  5.9 0.0 copy-done
  5.9 0.0 copy-done.2
  6.0 0.1 fusion.3
  6.1 0.5 copy.10
  6.6 0.9 pad_maximum_fusion
  7.6 1.3 gather_fusion
  8.9 0.0 copy-start.3
  8.9 0.0 copy-start.6
  8.9 0.3 fusion
  9.2 6.4 %collective-permute-start = (f32[4,256,256]{2,1,0:T(8,128)S(1)}, f32[4,256,256]{2,1,0:T(8,128)S(1)}, u32[]{:S(2)}, u32[]{:S(2)}) collective-permute-start(f32[4,256,256]{2,1,0:T(8,128)S(1)} %fusion), channel_id=1, source_target_pairs={{1,0},{2,1},{3,2},{4,3},{5,4},{6,5},{7,6},{8,7},{9,8},{10,9},{11,1... | collective-permute-start | bytes 3145736 | tf_op jit(solution)/shard_map/ppermute | solution.py:358
  15.6 2.6 %collective-permute-start.1 = (s32[256]{0:T(256)S(1)}, s32[256]{0:T(256)S(1)}, u32[]{:S(2)}, u32[]{:S(2)}) collective-permute-start(s32[256]{0:T(256)S(1)} %get-tuple-element.15), channel_id=1, source_target_pairs={{1,0},{2,1},{3,2},{4,3},{5,4},{6,5},{7,6},{8,7},{9,8},{10,9},{11,1... | collective-permute-start | bytes 3080 | tf_op jit(solution)/shard_map/ppermute | solution.py:358
  18.2 0.0 copy-done.3
  18.2 1.0 fusion.2.q
  19.2 0.0 copy-done.6
  19.2 0.8 jit_solution_.3.shift
  20.0 97.7 %local.1 = (f32[1025,8,128]{2,1,0:T(8,128)}, bf16[1025,32,128]{2,1,0:T(8,128)(2,1)}, bf16[1025,16,128]{2,1,0:T(8,128)(2,1)}) custom-call(f32[3,512,256]{2,1,0:T(8,128)} %pos.3, f32[512,256]{1,0:T(8,128)} %fusion.2.q, s32[512]{0:T(512)} %counts.3, s32[3,896]{1,0:T(4,128)} %pairs.3, bf16[27,16,128]{2,1,0:T(8,128)(2,1)} %constant.37.clone.scale, ...), custom_call_target="tpu_custom_call" | custom-call | tf_op jit(solution)/shard_map/local/pallas_call | solution.py:317
  117.7 0.0 collective-permute-done.1.rcounts
  117.7 0.0 copy-start.7
  117.7 0.0 collective-permute-done.rpos
  117.8 0.0 copy-start.5
  117.8 0.5 copy-done.7
  118.3 0.4 copy-done.5
  118.7 0.0 copy-start.1
  118.7 58.5 %remote.1 = (f32[1025,8,128]{2,1,0:T(8,128)}, f32[4,256,256]{2,1,0:T(8,128)}) custom-call(f32[4,256,256]{2,1,0:T(8,128)} %copy-done.5, s32[512]{0:T(512)} %counts.3, s32[256]{0:T(256)} %copy-done.7, s32[3,896]{1,0:T(4,128)} %pairs.3, bf16[27,16,128]{2,1,0:T(8,128)(2,1)} %constant.37.clone.scale, bf16[27,16,128]{2,1,0:T(8,128)(2,1)} %constant.38.clone.const, ...), custom_call_target="tpu_custom_call" | custom-call | tf_op jit(solution)/shard_map/remote/pallas_call | solution.py:334
  177.2 1.9 collective-permute-start.2
  179.1 0.0 copy-done.1
  179.1 1.0 fusion.1.occupied
  180.1 17.6 %collective-permute-done.2.back = f32[4,256,256]{2,1,0:T(8,128)S(1)} collective-permute-done((f32[4,256,256]{2,1,0:T(8,128)}, f32[4,256,256]{2,1,0:T(8,128)S(1)}, u32[]{:S(2)}, u32[]{:S(2)}) %collective-permute-start.2) | collective-permute-done | bytes 1048608 | tf_op jit(solution)/shard_map/ppermute | solution.py:358
  197.7 0.0 copy-start.4
  197.7 1.0 copy-done.4
  198.7 9.3 %final.1 = f32[4,512,256]{2,1,0:T(8,128)} custom-call(f32[1025,8,128]{2,1,0:T(8,128)} %get-tuple-element.13.acc, f32[3,512,256]{2,1,0:T(8,128)} %pos.3, f32[512,256]{1,0:T(8,128)} %fusion.2.q, f32[512,256]{1,0:T(8,128)} %fusion.1.occupied, s32[256]{0:T(256)} %send.1, f32[4,256,256]{2,1,0:T(8,128)} %copy-done.4), custom_call_target="tpu_custom_call" | custom-call | tf_op jit(solution)/shard_map/final/pallas_call | solution.py:349
  (1 shorter events, 0.0 us)
Async XLA Ops:
  2.7 3.3 %copy-start = (s32[512]{0:T(512)S(1)}, s32[512]{0:T(512)}, u32[]{:S(2)}) copy-start(s32[512]{0:T(512)} %counts.3) | copy-start | bytes 6148
  2.7 3.3 %copy-start.2 = (f32[512,256]{1,0:T(8,128)S(1)}, f32[512,256]{1,0:T(8,128)}, u32[]{:S(2)}) copy-start(f32[512,256]{1,0:T(8,128)} %param.9) | copy-start | bytes 1572868
  8.9 9.3 %copy-start.3 = (f32[512,256]{1,0:T(8,128)S(1)}, f32[512,256]{1,0:T(8,128)}, u32[]{:S(2)}) copy-start(f32[512,256]{1,0:T(8,128)} %param.9) | copy-start | bytes 1572868
  8.9 10.3 %copy-start.6 = (f32[27,16]{1,0:T(8,128)S(1)}, f32[27,16]{1,0:T(8,128)}, u32[]{:S(2)}) copy-start(f32[27,16]{1,0:T(8,128)} %constant.39.clone) | copy-start | bytes 5188
  9.2 108.5 %collective-permute-start = (f32[4,256,256]{2,1,0:T(8,128)S(1)}, f32[4,256,256]{2,1,0:T(8,128)S(1)}, u32[]{:S(2)}, u32[]{:S(2)}) collective-permute-start(f32[4,256,256]{2,1,0:T(8,128)S(1)} %fusion), channel_id=1, source_target_pairs={{1,0},{2,1},{3,2},{4,3},{5,4},{6,5},{7,6},{8,7},{9,8},{10,9},{11,1... | collective-permute-start | bytes 3145736 | tf_op jit(solution)/shard_map/ppermute | solution.py:358
  15.6 102.1 %collective-permute-start.1 = (s32[256]{0:T(256)S(1)}, s32[256]{0:T(256)S(1)}, u32[]{:S(2)}, u32[]{:S(2)}) collective-permute-start(s32[256]{0:T(256)S(1)} %get-tuple-element.15), channel_id=1, source_target_pairs={{1,0},{2,1},{3,2},{4,3},{5,4},{6,5},{7,6},{8,7},{9,8},{10,9},{11,1... | collective-permute-start | bytes 3080 | tf_op jit(solution)/shard_map/ppermute | solution.py:358
  117.7 0.6 copy-start.7
  117.8 1.0 copy-start.5
  118.7 60.4 %copy-start.1 = (s32[512]{0:T(512)S(1)}, s32[512]{0:T(512)}, u32[]{:S(2)}) copy-start(s32[512]{0:T(512)} %counts.3) | copy-start | bytes 6148
  177.2 20.5 %collective-permute-start.2 = (f32[4,256,256]{2,1,0:T(8,128)}, f32[4,256,256]{2,1,0:T(8,128)S(1)}, u32[]{:S(2)}, u32[]{:S(2)}) collective-permute-start(f32[4,256,256]{2,1,0:T(8,128)} %get-tuple-element.14), channel_id=1, source_target_pairs={{0,1},{1,2},{2,3},{3,4},{4,5},{5,6},{6,7},{7,8},{8,9},{9,10},{10,1... | collective-permute-start | bytes 3145736 | tf_op jit(solution)/shard_map/ppermute | solution.py:358
  197.7 1.0 copy-start.4

commit v2 on v1

v2 whole, which is shorter than its diff:
```python
import functools
import numpy as np
import jax, jax.numpy as jnp
from jax import lax
from jax.experimental import pallas as pl
from jax.experimental.pallas import tpu as pltpu
from jax.sharding import PartitionSpec as P

F32 = jnp.float32
BF16 = jnp.bfloat16
SOFTEN = 0.05
CELL = 128
STEPS = 4
NN = (((1,), (0,)), ((), ()))
TN = (((0,), (0,)), ((), ()))


def offset_tables():
    code = np.arange(27)
    o = np.stack([code // 9 - 1, code // 3 % 3 - 1, code % 3 - 1], 1).astype(np.float32)
    scale = np.zeros((27, 16), np.float32)
    scale[:, 0:3] = 2 * o
    scale[:, 8:11] = 2 * o
    const = np.zeros((27, 16), np.float32)
    const[:, 3] = (o * o).sum(1)
    const[:, 4:7] = o
    const[:, 15] = 1
    const[:, 12:15] = o
    shift = np.zeros((27, 16), np.float32)
    shift[:, 0:3] = o
    shift[:, 4:7] = o * o
    shift[:, 12:15] = 2 * o
    wide = lambda t: np.broadcast_to(t[:, :, None], t.shape + (CELL,))
    return (jnp.asarray(wide(np.concatenate([scale, const], 1)), BF16),
            jnp.asarray(wide(np.concatenate([shift, shift[::-1]], 1)), F32))


def rounded(x):
    return x.astype(BF16).astype(F32)


def two_parts(x):
    high = rounded(x)
    return high, rounded(x - high)


def three_parts(x):
    high, middle = two_parts(x)
    return high, middle, x - high - middle


def features(pos, q, rows):
    highs, mids, coords = [], [], []
    for x in pos:
        high, mid = two_parts(x - 0.5)
        highs.append(high)
        mids.append(mid)
        coords.append(high + mid)
    squares = [c * c for c in coords]
    norm = squares[0] + squares[1] + squares[2]

    def put(part, row, value):
        rows[part, pl.ds(row, 8, stride=8), :] = value

    s = three_parts(norm)
    for i in range(3):
        for base in (0, 4):
            put(0, base + i, highs[i])
            put(1, base + i, mids[i])
    put(0, 3, jnp.ones_like(q))
    put(0, 7, s[0])
    put(1, 3, s[2])
    put(1, 7, s[1])
    for i in range(3):
        for row, value in ((i, coords[i]), (4 + i, squares[i])):
            high, mid = two_parts(q * value)
            put(2, row, high)
            put(3, row, mid)
    high, mid = two_parts(q)
    put(2, 3, high)
    put(3, 3, mid)
    put(2, 7, jnp.zeros_like(q))
    put(3, 7, jnp.zeros_like(q))
    if rows.shape[0] > 4:
        n = two_parts(norm + SOFTEN)
        for i in range(3):
            put(4, i, -2.0 * highs[i])
            put(4, 4 + i, -2.0 * mids[i])
        put(4, 3, n[0])
        put(4, 7, n[1])


def prepare(pos_at, q_at, leaves, slots, stage, R, Q, L):
    row = lax.broadcasted_iota(jnp.int32, (8, CELL), 0)
    coordinate = (row & 3) < 3

    @pl.loop(0, lax.div(leaves, 8))
    def _(g):
        first = pl.multiple_of(g * 8, 8)
        for h in range(slots // CELL):
            lanes = slice(h * CELL, (h + 1) * CELL)
            pos = [pos_at(i, pl.ds(first, 8), lanes) for i in range(3)]
            q = q_at(pl.ds(first, 8), lanes)
            features(pos, q, stage.at[h])
            for k in range(8):
                to = h * leaves + first + k
                at = slice(8 * k, 8 * k + 8)
                R[to] = jnp.concatenate([stage[h, 0, at, :], stage[h, 1, at, :]], 0).astype(BF16)
                Q[to] = jnp.concatenate([stage[h, 2, at, :], stage[h, 3, at, :]], 0).astype(BF16)
                if L is not None:
                    x = stage[h, 4, at, :]
                    first_half = jnp.where(row == 7, 1.0, x)
                    second = jnp.where(coordinate, x, 1.0)
                    third = jnp.where((row > 3) & (row < 7), pltpu.roll(x, 4, 0), 1.0)
                    fourth = jnp.where(row > 3, x, 1.0)
                    L[to] = jnp.concatenate([first_half, second, third, fourth], 0).astype(BF16)


def finish_list(lists, n, U, values):
    @pl.loop(0, (5 + STEPS) * U)
    def _(i):
        for r, v in zip(lists, values):
            r[n + i] = v


def pipeline(U, batches, aim, gram_operands, aimed, gram, weights, turned, last, middle):
    def step(j):
        if last is not None:
            for k in range(U):
                last(j * U + k, turned[k])
        for k in range(U):
            w = weights[k]
            middle((j + 1) * U + k, w)
            if last is not None:
                turned[k, 0:CELL] = w[0:CELL].T
                turned[k, CELL:] = w[CELL:].T
        for k in range(U):
            w = lax.rsqrt(gram[k])
            w3 = w * w * w
            high = w3.astype(BF16)
            weights[k, 0:CELL] = high
            weights[k, CELL:] = (w3 - high.astype(F32)).astype(BF16)
        for k in range(U):
            gram[k] = lax.dot_general(aimed[k], gram_operands((j + 3) * U + k), NN, preferred_element_type=F32)
        for k in range(U):
            aimed[k] = aim((j + 4) * U + k).T

    @pl.loop(0, lax.div(batches + 3 + STEPS, STEPS))
    def _(i):
        for s in range(STEPS):
            step(i * STEPS + s)


def summed(q, w):
    out = lax.dot_general(jnp.concatenate([q, q], 1), w, NN, preferred_element_type=F32)
    return out[0:8] + out[8:16]


def moved(m, shift, code, base):
    total = jnp.broadcast_to(m[3:4], m.shape)
    return m + shift[code, base : base + 8] * total + shift[code, base + 8 : base + 16] * pltpu.roll(m, 4, 0)


def cross_cells(U, lists, n, table, shift, L, Qa, acc_a, R, Qb, acc_b, scratch):
    la, lb, lc = lists

    def operands(i):
        b, c = lb[i], lc[i]
        r0 = R[b]
        return jnp.concatenate([r0, r0 * table[c, 0:16] + table[c, 16:32]], 0)

    def on_source(i, w):
        acc_b[lb[i]] += moved(summed(Qa[la[i]], w), shift, lc[i], 16)

    def on_target(i, w):
        acc_a[la[i]] += moved(summed(Qb[lb[i]], w), shift, lc[i], 0)

    pipeline(U, lax.div(n - 4 * U + U - 1, U), lambda i: L[la[i]], operands, *scratch, on_target, on_source)


def own_cells(U, cells, n, table, L, R, Q, acc, scratch):
    def operands(i):
        return jnp.concatenate([R[cells[i]], table[13, 16:32]], 0)

    def on_target(i, w):
        acc[cells[i]] += summed(Q[cells[i]], w)

    pipeline(U, lax.div(n - 4 * U + U - 1, U), lambda i: L[cells[i]], operands, *scratch, None, on_target)


def clear(aimed, gram, weights, turned):
    aimed[...] = jnp.zeros_like(aimed)
    gram[...] = jnp.ones_like(gram)
    weights[...] = jnp.zeros_like(weights)
    turned[...] = jnp.zeros_like(turned)


def start_list(lists, U, values):
    for r, v in zip(lists, values):
        for k in range(4 * U):
            r[k] = v


def list_pairs(lists, n, pairs, first, count, second_base, counts_a, counts_b, half_a, half_b):
    la, lb, lc = lists

    def body(i, n):
        a, b, code = pairs[0, i], pairs[1, i] - second_base, pairs[2, i]
        more_a = (counts_a[a] > CELL).astype(jnp.int32)
        more_b = (counts_b[b] > CELL).astype(jnp.int32)
        for da, db, more in ((0, 0, 1), (half_a, 0, more_a), (0, half_b, more_b), (half_a, half_b, more_a * more_b)):
            la[n] = a + da
            lb[n] = b + db
            lc[n] = code
            n = n + more
        return n

    return lax.fori_loop(first, first + count, body, n, unroll=4)


def idle_cell(L, R, Q, at_l, at_r):
    if L is not None:
        L[at_l] = jnp.ones(L.shape[1:], BF16)
    R[at_r] = jnp.zeros(R.shape[1:], BF16)
    Q[at_r] = jnp.zeros(Q.shape[1:], BF16)


def local_kernel(U, leaves, slots, npairs, pos, q, counts, pairs, table, shift, acc, L, Q, R, stage, own, la, lb, lc, *scratch):
    dummy = 2 * leaves
    lists = (la, lb, lc)
    acc[...] = jnp.zeros_like(acc)
    idle_cell(L, R, Q, dummy, dummy)
    clear(*scratch)
    start_list((own,), U, (dummy,))
    start_list(lists, U, (dummy, dummy, 13))
    prepare(lambda i, r, s: pos[i, r, s], lambda r, s: q[r, s], leaves, slots, stage, R, Q, L)

    def body(l, carry):
        n, nx = carry
        more = (counts[l] > CELL).astype(jnp.int32)
        own[n] = l
        own[n + 1] = l + leaves
        la[nx] = l
        lb[nx] = l + leaves
        lc[nx] = 13
        return n + 1 + more, nx + more

    n, nx = lax.fori_loop(0, leaves, body, (4 * U, 4 * U), unroll=8)
    nx = list_pairs(lists, nx, pairs, leaves, npairs, 0, counts, counts, leaves, leaves)
    finish_list((own,), n, U, (dummy,))
    finish_list(lists, nx, U, (dummy, dummy, 13))
    own_cells(U, own, n, table, L, R, Q, acc, scratch)
    clear(*scratch)
    cross_cells(U, lists, nx, table, shift, L, Q, acc, R, Q, acc, scratch)


def remote_kernel(U, leaves, remotes, slots, npairs, first, rpos, counts, rcounts, pairs, table, shift, L, Qa, acc_in,
                  acc, back, R, Q, acc_b, stage, la, lb, lc, *scratch):
    dummy_a, dummy_b = 2 * leaves, 2 * remotes
    lists = (la, lb, lc)
    acc[...] = acc_in[...]
    acc_b[...] = jnp.zeros_like(acc_b)
    idle_cell(None, R, Q, dummy_a, dummy_b)
    clear(*scratch)
    start_list(lists, U, (dummy_a, dummy_b, 13))
    prepare(lambda i, r, s: rpos[i, r, s], lambda r, s: rpos[3, r, s], remotes, slots, stage, R, Q, None)
    nx = list_pairs(lists, 4 * U, pairs, first, npairs, leaves, counts, rcounts, leaves, remotes)
    finish_list(lists, nx, U, (dummy_a, dummy_b, 13))
    cross_cells(U, lists, nx, table, shift, L, Qa, acc, R, Q, acc_b, scratch)

    @pl.loop(0, remotes // 8)
    def _(g):
        r = pl.ds(pl.multiple_of(g * 8, 8), 8)
        for h in range(slots // CELL):
            lanes = slice(h * CELL, (h + 1) * CELL)
            cells = pl.ds(pl.multiple_of(h * remotes + g * 8, 8), 8)
            values = finished(acc_b, cells, [rpos[i, r, lanes] for i in range(3)])
            for i in range(4):
                back[i, r, lanes] = values[i]


def finished(acc, cells, pos):
    u = [sum(two_parts(x - 0.5)) for x in pos]
    total = acc[cells, 3, :]
    moments = [acc[cells, i, :] for i in range(3)]
    square = acc[cells, 4, :] + acc[cells, 5, :] + acc[cells, 6, :]
    norm = u[0] * u[0] + u[1] * u[1] + u[2] * u[2]
    dots = u[0] * moments[0] + u[1] * moments[1] + u[2] * moments[2]
    phi = (norm + SOFTEN) * total - 2.0 * dots + square
    return [phi] + [u[i] * total - moments[i] for i in range(3)]


def final_kernel(leaves, remotes, slots, acc, pos, q, occupied, send, back, out):
    @pl.loop(0, leaves // 8)
    def _(g):
        r = pl.ds(pl.multiple_of(g * 8, 8), 8)
        for h in range(slots // CELL):
            lanes = slice(h * CELL, (h + 1) * CELL)
            cells = pl.ds(pl.multiple_of(h * leaves + g * 8, 8), 8)
            values = finished(acc, cells, [pos[i, r, lanes] for i in range(3)])
            values[0] = values[0] - q[r, lanes] * (1.0 / np.sqrt(SOFTEN))
            for i in range(4):
                out[i, r, lanes] = values[i]

    if send is not None:
        def give(k, _):
            l = send[k]
            for i in range(4):
                out[i, pl.ds(l, 1), :] += back[i, pl.ds(k, 1), :]
            return 0
        lax.fori_loop(0, remotes, give, 0, unroll=8)

    @pl.loop(0, leaves // 8)
    def _(g):
        r = pl.ds(pl.multiple_of(g * 8, 8), 8)
        for i in range(4):
            out[i, r, :] = out[i, r, :] * occupied[r, :]


SMEM = pl.BlockSpec(memory_space=pltpu.SMEM)
VMEM = pl.BlockSpec(memory_space=pltpu.VMEM)
PARAMS = pltpu.CompilerParams(vmem_limit_bytes=58 << 20)


def scratch_loop(U):
    return [pltpu.VMEM((U, CELL, 32), BF16), pltpu.VMEM((U, CELL, CELL), F32)] + [pltpu.VMEM((U, 2 * CELL, CELL), BF16)] * 2


def local_call(U, pos, q, counts, pairs, tables, npairs):
    leaves, slots = q.shape
    cells = 2 * leaves + 1
    return pl.pallas_call(
        functools.partial(local_kernel, U, leaves, slots, npairs),
        out_shape=(jax.ShapeDtypeStruct((cells, 8, CELL), F32), jax.ShapeDtypeStruct((cells, 32, CELL), BF16),
                   jax.ShapeDtypeStruct((cells, 16, CELL), BF16)),
        in_specs=[VMEM, VMEM, SMEM, SMEM, VMEM, VMEM],
        out_specs=(VMEM, VMEM, VMEM),
        scratch_shapes=[pltpu.VMEM((cells, 16, CELL), BF16), pltpu.VMEM((2, 5, 64, CELL), F32),
                        pltpu.SMEM((2 * leaves + (10 + STEPS) * U,), jnp.int32)]
        + [pltpu.SMEM((leaves + 4 * npairs + (10 + STEPS) * U,), jnp.int32)] * 3 + scratch_loop(U),
        compiler_params=PARAMS, name="local")(pos, q, counts, pairs, *tables)


def remote_call(U, rpos, counts, rcounts, pairs, tables, L, Q, acc, first, npairs):
    leaves = counts.shape[0]
    remotes, slots = rpos.shape[1:]
    cells = 2 * remotes + 1
    return pl.pallas_call(
        functools.partial(remote_kernel, U, leaves, remotes, slots, npairs, first),
        out_shape=(jax.ShapeDtypeStruct(acc.shape, F32), jax.ShapeDtypeStruct(rpos.shape, F32)),
        in_specs=[VMEM, SMEM, SMEM, SMEM, VMEM, VMEM, VMEM, VMEM, VMEM],
        out_specs=(VMEM, VMEM),
        scratch_shapes=[pltpu.VMEM((cells, 16, CELL), BF16), pltpu.VMEM((cells, 16, CELL), BF16),
                        pltpu.VMEM((cells, 8, CELL), F32), pltpu.VMEM((2, 4, 64, CELL), F32)]
        + [pltpu.SMEM((4 * npairs + (10 + STEPS) * U,), jnp.int32)] * 3 + scratch_loop(U),
        compiler_params=PARAMS, name="remote")(rpos, counts, rcounts, pairs, *tables, L, Q, acc)


def final_call(acc, pos, q, occupied, send, back):
    leaves, slots = q.shape
    remotes = back.shape[1]
    return pl.pallas_call(
        functools.partial(final_kernel, leaves, remotes, slots),
        out_shape=jax.ShapeDtypeStruct((4, leaves, slots), F32),
        in_specs=[VMEM, VMEM, VMEM, VMEM, SMEM, VMEM], out_specs=VMEM,
        compiler_params=PARAMS, name="final")(acc, pos, q, occupied, send, back)


def shifted(value, axis, by):
    length = lax.axis_size(axis)
    return lax.ppermute(value, axis, [(i, i + by) for i in range(length) if 0 <= i + by < length])


AXES = ("leaf", "grp")
GROUP = 8


def on_device(positions, charges, counts, send_left, pairs):
    leaves, slots = charges.shape
    remotes = send_left.shape[0]
    near = pairs.shape[1] - leaves - remotes
    occupied = (jnp.arange(slots)[None, :] < counts[:, None]).astype(jnp.float32)
    charges = charges * occupied
    tables = offset_tables()
    outgoing = jnp.take(jnp.concatenate([positions, charges[None]], 0), send_left, axis=1)
    remote = shifted(outgoing, AXES, -1)
    remote_counts = shifted(jnp.take(counts, send_left), AXES, -1)
    acc, L, Q = local_call(GROUP, positions, charges, counts, pairs, tables, near)
    acc, back = remote_call(GROUP, remote, counts, remote_counts, pairs, tables, L, Q, acc, leaves + near, remotes)
    returned = shifted(back, AXES, 1)
    return final_call(acc, positions, charges, occupied, send_left, returned)


def solution(mesh):
    in_specs = (P(None, AXES, None), P(AXES, None), P(AXES), P(AXES), P(None, AXES))
    return jax.shard_map(on_device, mesh=mesh, in_specs=in_specs, out_specs=P(None, AXES, None), check_vma=False)
```

time: 208 us -> 182 us (0.88)
  Pallas kernels: 166 us -> 138 us
    pallas_call x1, Pallas kernels: 97.7 us -> 78.2 us  [local_call(): pl.pallas_call(functools.partial(local_kernel, U, leaves, slots, npairs),...]
    pallas_call x1, Pallas kernels: 58.5 us -> 50.9 us  [remote_call(): pl.pallas_call(functools.partial(remote_kernel, U, leaves, remotes, slots...]
  transfers between devices with their start and end apart: 3 -> 3, of which waited for: 1 -> 1; matrix products, arithmetic and copies ran while one was open for 1% -> 2% of each run, Pallas kernels for 47% -> 43%
where the time goes in v2:
time: 182 us; the launch traced here: 181 us
  Pallas kernels  138 us (76%)
  waiting for transfers between devices  16.6 us (9%)
  starting transfers between devices  12 us (7%)
  local copies, waits for them, and re-layouts  9.19 us (5%)
  other arithmetic  4.74 us (3%)
    pallas_call x1, Pallas kernels, local_call(): pl.pallas_call(functools.partial(local_kernel, U, leaves, slots, npairs),...  78.2 us
    pallas_call x1, Pallas kernels, remote_call(): pl.pallas_call(functools.partial(remote_kernel, U, leaves, remotes, slots...  50.9 us
    ppermute x3, waiting for transfers between devices, shifted(): lax.ppermute(value, axis, [(i, i + by) for i in range(length) if 0 <= i +...  16.6 us
    ppermute x3, starting transfers between devices, shifted(): lax.ppermute(value, axis, [(i, i + by) for i in range(length) if 0 <= i +...  12 us
    pallas_call x1, Pallas kernels, final_call(): pl.pallas_call(functools.partial(final_kernel, leaves, remotes, slots), o...  9.32 us
    unnamed x17, local copies, waits for them, and re-layouts  4.45 us
  transfers between devices with their start and end apart: 3, of which 1 were waited for; matrix products, arithmetic and copies ran while one was open for 2% of the time, Pallas kernels for 43%

profile of v2, /device:TPU:96, one launch (start us, length us, event | category | flops | bytes accessed | tf_op | source)
XLA Modules:
  0.0 181.0 jit_solution(11128522089511803383)
XLA Ops:
  0.0 0.7 compare_select_fusion
  0.7 2.0 %gather_fusion.1 = s32[256]{0:T(256)S(1)} fusion(s32[512]{0:T(512)} %counts.3, s32[1024]{0:T(1024)S(1)} %pad_clamp_fusion), kind=kCustom, calls=%fused_computation.1 | custom fusion | bytes 3072 | tf_op jit(solution)/shard_map/jit(_take)/gather | solution.py:387
  2.7 0.0 copy-start
  2.7 0.0 copy-start.2
  2.7 0.7 broadcast_select_fusion
  3.4 2.5 %copy.8 = f32[3,512,256]{2,0,1:T(4,128)S(1)} copy(f32[3,512,256]{2,1,0:T(8,128)} %pos.3) | data formatting | bytes 3145728 | tf_op args[0]
  5.9 0.0 copy-done
  5.9 0.0 copy-done.2
  6.0 0.1 fusion.3
  6.1 0.5 copy.9
  6.6 0.9 pad_maximum_fusion
  7.6 1.3 gather_fusion
  8.9 0.0 copy-start.3
  8.9 0.0 copy-start.6
  8.9 0.3 fusion
  9.2 6.4 %collective-permute-start = (f32[4,256,256]{2,1,0:T(8,128)S(1)}, f32[4,256,256]{2,1,0:T(8,128)S(1)}, u32[]{:S(2)}, u32[]{:S(2)}) collective-permute-start(f32[4,256,256]{2,1,0:T(8,128)S(1)} %fusion), channel_id=1, source_target_pairs={{1,0},{2,1},{3,2},{4,3},{5,4},{6,5},{7,6},{8,7},{9,8},{10,9},{11,1... | collective-permute-start | bytes 3145736 | tf_op jit(solution)/shard_map/ppermute | solution.py:371
  15.6 2.6 %collective-permute-start.1 = (s32[256]{0:T(256)S(1)}, s32[256]{0:T(256)S(1)}, u32[]{:S(2)}, u32[]{:S(2)}) collective-permute-start(s32[256]{0:T(256)S(1)} %get-tuple-element.15), channel_id=1, source_target_pairs={{1,0},{2,1},{3,2},{4,3},{5,4},{6,5},{7,6},{8,7},{9,8},{10,9},{11,1... | collective-permute-start | bytes 3080 | tf_op jit(solution)/shard_map/ppermute | solution.py:371
  18.2 0.0 copy-done.3
  18.2 1.0 fusion.2.q
  19.2 0.0 copy-done.6
  19.2 0.9 jit_solution_.3.shift
  20.1 78.2 %local.1 = (f32[1025,8,128]{2,1,0:T(8,128)}, bf16[1025,32,128]{2,1,0:T(8,128)(2,1)}, bf16[1025,16,128]{2,1,0:T(8,128)(2,1)}) custom-call(f32[3,512,256]{2,1,0:T(8,128)} %pos.3, f32[512,256]{1,0:T(8,128)} %fusion.2.q, s32[512]{0:T(512)} %counts.3, s32[3,896]{1,0:T(4,128)} %pairs.3, bf16[27,32,128]{2,1,0:T(8,128)(2,1)} %constant.35.clone.table, ...), custom_call_target="tpu_custom_call" | custom-call | tf_op jit(solution)/shard_map/local/pallas_call | solution.py:332
  98.3 0.0 collective-permute-done.1.rcounts
  98.3 0.0 copy-start.7
  98.3 0.0 collective-permute-done.rpos
  98.3 0.0 copy-start.4
  98.3 0.5 copy-done.7
  98.8 0.4 copy-done.4
  99.3 0.0 copy-start.1
  99.3 50.9 %remote.1 = (f32[1025,8,128]{2,1,0:T(8,128)}, f32[4,256,256]{2,1,0:T(8,128)}) custom-call(f32[4,256,256]{2,1,0:T(8,128)} %copy-done.4, s32[512]{0:T(512)} %counts.3, s32[256]{0:T(256)} %copy-done.7, s32[3,896]{1,0:T(4,128)} %pairs.3, bf16[27,32,128]{2,1,0:T(8,128)(2,1)} %constant.35.clone.table, f32[27,32,128]{2,1,0:T(8,128)} %jit_solution_.3.shift, ...), custom_call_target="tpu_custom_call" | custom-call | tf_op jit(solution)/shard_map/remote/pallas_call | solution.py:348
  150.2 3.0 %collective-permute-start.2 = (f32[4,256,256]{2,1,0:T(8,128)}, f32[4,256,256]{2,1,0:T(8,128)S(1)}, u32[]{:S(2)}, u32[]{:S(2)}) collective-permute-start(f32[4,256,256]{2,1,0:T(8,128)} %get-tuple-element.14), channel_id=1, source_target_pairs={{0,1},{1,2},{2,3},{3,4},{4,5},{5,6},{6,7},{7,8},{8,9},{9,10},{10,1... | collective-permute-start | bytes 3145736 | tf_op jit(solution)/shard_map/ppermute | solution.py:371
  153.2 0.0 copy-done.1
  153.2 1.0 fusion.1.occupied
  154.1 16.6 %collective-permute-done.2.back = f32[4,256,256]{2,1,0:T(8,128)S(1)} collective-permute-done((f32[4,256,256]{2,1,0:T(8,128)}, f32[4,256,256]{2,1,0:T(8,128)S(1)}, u32[]{:S(2)}, u32[]{:S(2)}) %collective-permute-start.2) | collective-permute-done | bytes 1048608 | tf_op jit(solution)/shard_map/ppermute | solution.py:371
  170.7 0.0 copy-start.5
  170.7 1.0 copy-done.5
  171.7 9.3 %final.1 = f32[4,512,256]{2,1,0:T(8,128)} custom-call(f32[1025,8,128]{2,1,0:T(8,128)} %get-tuple-element.13.acc, f32[3,512,256]{2,1,0:T(8,128)} %pos.3, f32[512,256]{1,0:T(8,128)} %fusion.2.q, f32[512,256]{1,0:T(8,128)} %fusion.1.occupied, s32[256]{0:T(256)} %send.1, f32[4,256,256]{2,1,0:T(8,128)} %copy-done.5), custom_call_target="tpu_custom_call" | custom-call | tf_op jit(solution)/shard_map/final/pallas_call | solution.py:362
  (1 shorter events, 0.0 us)
Async XLA Ops:
  2.7 3.3 %copy-start = (s32[512]{0:T(512)S(1)}, s32[512]{0:T(512)}, u32[]{:S(2)}) copy-start(s32[512]{0:T(512)} %counts.3) | copy-start | bytes 6148
  2.7 3.3 %copy-start.2 = (f32[512,256]{1,0:T(8,128)S(1)}, f32[512,256]{1,0:T(8,128)}, u32[]{:S(2)}) copy-start(f32[512,256]{1,0:T(8,128)} %param.8) | copy-start | bytes 1572868
  8.9 9.3 %copy-start.3 = (f32[512,256]{1,0:T(8,128)S(1)}, f32[512,256]{1,0:T(8,128)}, u32[]{:S(2)}) copy-start(f32[512,256]{1,0:T(8,128)} %param.8) | copy-start | bytes 1572868
  8.9 10.3 %copy-start.6 = (f32[27,32]{1,0:T(8,128)S(1)}, f32[27,32]{1,0:T(8,128)}, u32[]{:S(2)}) copy-start(f32[27,32]{1,0:T(8,128)} %constant.36.clone) | copy-start | bytes 10372
  9.2 89.1 %collective-permute-start = (f32[4,256,256]{2,1,0:T(8,128)S(1)}, f32[4,256,256]{2,1,0:T(8,128)S(1)}, u32[]{:S(2)}, u32[]{:S(2)}) collective-permute-start(f32[4,256,256]{2,1,0:T(8,128)S(1)} %fusion), channel_id=1, source_target_pairs={{1,0},{2,1},{3,2},{4,3},{5,4},{6,5},{7,6},{8,7},{9,8},{10,9},{11,1... | collective-permute-start | bytes 3145736 | tf_op jit(solution)/shard_map/ppermute | solution.py:371
  15.6 82.7 %collective-permute-start.1 = (s32[256]{0:T(256)S(1)}, s32[256]{0:T(256)S(1)}, u32[]{:S(2)}, u32[]{:S(2)}) collective-permute-start(s32[256]{0:T(256)S(1)} %get-tuple-element.15), channel_id=1, source_target_pairs={{1,0},{2,1},{3,2},{4,3},{5,4},{6,5},{7,6},{8,7},{9,8},{10,9},{11,1... | collective-permute-start | bytes 3080 | tf_op jit(solution)/shard_map/ppermute | solution.py:371
  98.3 0.5 copy-start.7
  98.3 1.0 copy-start.4
  99.3 53.9 %copy-start.1 = (s32[512]{0:T(512)S(1)}, s32[512]{0:T(512)}, u32[]{:S(2)}) copy-start(s32[512]{0:T(512)} %counts.3) | copy-start | bytes 6148
  150.2 20.5 %collective-permute-start.2 = (f32[4,256,256]{2,1,0:T(8,128)}, f32[4,256,256]{2,1,0:T(8,128)S(1)}, u32[]{:S(2)}, u32[]{:S(2)}) collective-permute-start(f32[4,256,256]{2,1,0:T(8,128)} %get-tuple-element.14), channel_id=1, source_target_pairs={{0,1},{1,2},{2,3},{3,4},{4,5},{5,6},{6,7},{7,8},{8,9},{9,10},{10,1... | collective-permute-start | bytes 3145736 | tf_op jit(solution)/shard_map/ppermute | solution.py:371
  170.7 1.0 copy-start.5

commit v3 on v2

--- a/solution.py
+++ b/solution.py
@@ -90,12 +90,12 @@
         put(4, 7, n[1])
 
 
-def prepare(pos_at, q_at, leaves, slots, stage, R, Q, L):
+def prepare(pos_at, q_at, leaves, slots, stage, R, Q, L, extra, carry):
     row = lax.broadcasted_iota(jnp.int32, (8, CELL), 0)
     coordinate = (row & 3) < 3
 
-    @pl.loop(0, lax.div(leaves, 8))
-    def _(g):
+    def body(g, carry):
+        carry = extra(g, carry)
         first = pl.multiple_of(g * 8, 8)
         for h in range(slots // CELL):
             lanes = slice(h * CELL, (h + 1) * CELL)
@@ -114,6 +114,9 @@
                     third = jnp.where((row > 3) & (row < 7), pltpu.roll(x, 4, 0), 1.0)
                     fourth = jnp.where(row > 3, x, 1.0)
                     L[to] = jnp.concatenate([first_half, second, third, fourth], 0).astype(BF16)
+        return carry
+
+    return lax.fori_loop(0, leaves // 8, body, carry)
 
 
 def finish_list(lists, n, U, values):
@@ -178,6 +181,22 @@
     pipeline(U, lax.div(n - 4 * U + U - 1, U), lambda i: L[la[i]], operands, *scratch, on_target, on_source)
 
 
+def half_cells(U, leaves, cells, n, table, L, R, Q, acc, scratch):
+    def second(i):
+        return jnp.minimum(cells[i] + leaves, 2 * leaves)
+
+    def operands(i):
+        return jnp.concatenate([R[second(i)], table[13, 16:32]], 0)
+
+    def on_source(i, w):
+        acc[second(i)] += summed(Q[cells[i]], w)
+
+    def on_target(i, w):
+        acc[cells[i]] += summed(Q[second(i)], w)
+
+    pipeline(U, lax.div(n - 4 * U + U - 1, U), lambda i: L[cells[i]], operands, *scratch, on_target, on_source)
+
+
 def own_cells(U, cells, n, table, L, R, Q, acc, scratch):
     def operands(i):
         return jnp.concatenate([R[cells[i]], table[13, 16:32]], 0)
@@ -201,21 +220,17 @@
             r[k] = v
 
 
-def list_pairs(lists, n, pairs, first, count, second_base, counts_a, counts_b, half_a, half_b):
+def list_pair(lists, n, pairs, i, second_base, counts_a, counts_b, half_a, half_b):
     la, lb, lc = lists
-
-    def body(i, n):
-        a, b, code = pairs[0, i], pairs[1, i] - second_base, pairs[2, i]
-        more_a = (counts_a[a] > CELL).astype(jnp.int32)
-        more_b = (counts_b[b] > CELL).astype(jnp.int32)
-        for da, db, more in ((0, 0, 1), (half_a, 0, more_a), (0, half_b, more_b), (half_a, half_b, more_a * more_b)):
-            la[n] = a + da
-            lb[n] = b + db
-            lc[n] = code
-            n = n + more
-        return n
-
-    return lax.fori_loop(first, first + count, body, n, unroll=4)
+    a, b, code = pairs[0, i], pairs[1, i] - second_base, pairs[2, i]
+    more_a = (counts_a[a] > CELL).astype(jnp.int32)
+    more_b = (counts_b[b] > CELL).astype(jnp.int32)
+    for da, db, more in ((0, 0, 1), (half_a, 0, more_a), (0, half_b, more_b), (half_a, half_b, more_a * more_b)):
+        la[n] = a + da
+        lb[n] = b + db
+        lc[n] = code
+        n = n + more
+    return n
 
 
 def idle_cell(L, R, Q, at_l, at_r):
@@ -225,46 +240,70 @@
     Q[at_r] = jnp.zeros(Q.shape[1:], BF16)
 
 
-def local_kernel(U, leaves, slots, npairs, pos, q, counts, pairs, table, shift, acc, L, Q, R, stage, own, la, lb, lc, *scratch):
+def local_kernel(U, leaves, slots, npairs, pos, q, counts, pairs, table, shift, acc, L, Q, R, own, half, sizes, stage, la, lb,
+                 lc, *scratch):
     dummy = 2 * leaves
     lists = (la, lb, lc)
     acc[...] = jnp.zeros_like(acc)
     idle_cell(L, R, Q, dummy, dummy)
     clear(*scratch)
-    start_list((own,), U, (dummy,))
+    start_list((own, half), U, (dummy, dummy))
     start_list(lists, U, (dummy, dummy, 13))
-    prepare(lambda i, r, s: pos[i, r, s], lambda r, s: q[r, s], leaves, slots, stage, R, Q, L)
-
-    def body(l, carry):
-        n, nx = carry
-        more = (counts[l] > CELL).astype(jnp.int32)
-        own[n] = l
-        own[n + 1] = l + leaves
-        la[nx] = l
-        lb[nx] = l + leaves
-        lc[nx] = 13
-        return n + 1 + more, nx + more
-
-    n, nx = lax.fori_loop(0, leaves, body, (4 * U, 4 * U), unroll=8)
-    nx = list_pairs(lists, nx, pairs, leaves, npairs, 0, counts, counts, leaves, leaves)
+    groups = leaves // 8
+    share = npairs // groups
+
+    def extra(g, carry):
+        n, nh, nx = carry
+        for k in range(8):
+            l = 8 * g + k
+            more = (counts[l] > CELL).astype(jnp.int32)
+            own[n] = l
+            own[n + 1] = l + leaves
+            half[nh] = l
+            n = n + 1 + more
+            nh = nh + more
+        for k in range(share):
+            nx = list_pair(lists, nx, pairs, leaves + g * share + k, 0, counts, counts, leaves, leaves)
+        return n, nh, nx
+
+    n, nh, nx = prepare(lambda i, r, s: pos[i, r, s], lambda r, s: q[r, s], leaves, slots, stage, R, Q, L, extra,
+                        (4 * U, 4 * U, 4 * U))
+    nx = lax.fori_loop(leaves + groups * share, leaves + npairs, lambda i, nx: list_pair(
+        lists, nx, pairs, i, 0, counts, counts, leaves, leaves), nx)
     finish_list((own,), n, U, (dummy,))
+    finish_list((half,), nh, U, (dummy,))
     finish_list(lists, nx, U, (dummy, dummy, 13))
-    own_cells(U, own, n, table, L, R, Q, acc, scratch)
+    sizes[0] = n
+    sizes[1] = nh
+    cross_cells(U, lists, nx, table, shift, L, Q, acc, R, Q, acc, scratch)
+
+
+def own_kernel(U, leaves, own, half, sizes, table, L, R, Q, acc_in, acc, *scratch):
     clear(*scratch)
-    cross_cells(U, lists, nx, table, shift, L, Q, acc, R, Q, acc, scratch)
+    half_cells(U, leaves, half, sizes[1], table, L, R, Q, acc, scratch)
+    clear(*scratch)
+    own_cells(U, own, sizes[0], table, L, R, Q, acc, scratch)
 
 
 def remote_kernel(U, leaves, remotes, slots, npairs, first, rpos, counts, rcounts, pairs, table, shift, L, Qa, acc_in,
                   acc, back, R, Q, acc_b, stage, la, lb, lc, *scratch):
     dummy_a, dummy_b = 2 * leaves, 2 * remotes
     lists = (la, lb, lc)
-    acc[...] = acc_in[...]
     acc_b[...] = jnp.zeros_like(acc_b)
     idle_cell(None, R, Q, dummy_a, dummy_b)
     clear(*scratch)
     start_list(lists, U, (dummy_a, dummy_b, 13))
-    prepare(lambda i, r, s: rpos[i, r, s], lambda r, s: rpos[3, r, s], remotes, slots, stage, R, Q, None)
-    nx = list_pairs(lists, 4 * U, pairs, first, npairs, leaves, counts, rcounts, leaves, remotes)
+    groups = remotes // 8
+    share = npairs // groups
+
+    def extra(g, nx):
+        for k in range(share):
+            nx = list_pair(lists, nx, pairs, first + g * share + k, leaves, counts, rcounts, leaves, remotes)
+        return nx
+
+    nx = prepare(lambda i, r, s: rpos[i, r, s], lambda r, s: rpos[3, r, s], remotes, slots, stage, R, Q, None, extra, 4 * U)
+    nx = lax.fori_loop(first + groups * share, first + npairs, lambda i, nx: list_pair(
+        lists, nx, pairs, i, leaves, counts, rcounts, leaves, remotes), nx)
     finish_list(lists, nx, U, (dummy_a, dummy_b, 13))
     cross_cells(U, lists, nx, table, shift, L, Qa, acc, R, Q, acc_b, scratch)
 
@@ -303,12 +342,16 @@
                 out[i, r, lanes] = values[i]
 
     if send is not None:
-        def give(k, _):
-            l = send[k]
+        def give(g, _):
+            rows = [pl.ds(send[8 * g + k], 1) for k in range(8)]
+            r = pl.ds(pl.multiple_of(g * 8, 8), 8)
             for i in range(4):
-                out[i, pl.ds(l, 1), :] += back[i, pl.ds(k, 1), :]
+                extra = back[i, r, :]
+                sums = [out[i, rows[k], :] + extra[k : k + 1] for k in range(8)]
+                for k in range(8):
+                    out[i, rows[k], :] = sums[k]
             return 0
-        lax.fori_loop(0, remotes, give, 0, unroll=8)
+        lax.fori_loop(0, remotes // 8, give, 0)
 
     @pl.loop(0, leaves // 8)
     def _(g):
@@ -319,25 +362,31 @@
 
 SMEM = pl.BlockSpec(memory_space=pltpu.SMEM)
 VMEM = pl.BlockSpec(memory_space=pltpu.VMEM)
-PARAMS = pltpu.CompilerParams(vmem_limit_bytes=58 << 20)
+PARAMS = pltpu.CompilerParams(vmem_limit_bytes=20 << 20)
 
 
 def scratch_loop(U):
     return [pltpu.VMEM((U, CELL, 32), BF16), pltpu.VMEM((U, CELL, CELL), F32)] + [pltpu.VMEM((U, 2 * CELL, CELL), BF16)] * 2
+
+
+def pinned(x):
+    return pltpu.with_memory_space_constraint(x, pltpu.VMEM)
 
 
 def local_call(U, pos, q, counts, pairs, tables, npairs):
     leaves, slots = q.shape
     cells = 2 * leaves + 1
+    room = (10 + STEPS) * U
     return pl.pallas_call(
         functools.partial(local_kernel, U, leaves, slots, npairs),
-        out_shape=(jax.ShapeDtypeStruct((cells, 8, CELL), F32), jax.ShapeDtypeStruct((cells, 32, CELL), BF16),
-                   jax.ShapeDtypeStruct((cells, 16, CELL), BF16)),
+        out_shape=(pltpu.VMEM((cells, 8, CELL), F32), pltpu.VMEM((cells, 32, CELL), BF16),
+                   pltpu.VMEM((cells, 16, CELL), BF16), pltpu.VMEM((cells, 16, CELL), BF16),
+                   jax.ShapeDtypeStruct((2 * leaves + room,), jnp.int32), jax.ShapeDtypeStruct((leaves + room,), jnp.int32),
+                   jax.ShapeDtypeStruct((2,), jnp.int32)),
         in_specs=[VMEM, VMEM, SMEM, SMEM, VMEM, VMEM],
-        out_specs=(VMEM, VMEM, VMEM),
-        scratch_shapes=[pltpu.VMEM((cells, 16, CELL), BF16), pltpu.VMEM((2, 5, 64, CELL), F32),
-                        pltpu.SMEM((2 * leaves + (10 + STEPS) * U,), jnp.int32)]
-        + [pltpu.SMEM((leaves + 4 * npairs + (10 + STEPS) * U,), jnp.int32)] * 3 + scratch_loop(U),
+        out_specs=(VMEM, VMEM, VMEM, VMEM, SMEM, SMEM, SMEM),
+        scratch_shapes=[pltpu.VMEM((2, 5, 64, CELL), F32)]
+        + [pltpu.SMEM((4 * npairs + room,), jnp.int32)] * 3 + scratch_loop(U),
         compiler_params=PARAMS, name="local")(pos, q, counts, pairs, *tables)
 
 
@@ -347,13 +396,22 @@
     cells = 2 * remotes + 1
     return pl.pallas_call(
         functools.partial(remote_kernel, U, leaves, remotes, slots, npairs, first),
-        out_shape=(jax.ShapeDtypeStruct(acc.shape, F32), jax.ShapeDtypeStruct(rpos.shape, F32)),
+        out_shape=(pltpu.VMEM(acc.shape, F32), jax.ShapeDtypeStruct(rpos.shape, F32)),
         in_specs=[VMEM, SMEM, SMEM, SMEM, VMEM, VMEM, VMEM, VMEM, VMEM],
-        out_specs=(VMEM, VMEM),
+        out_specs=(VMEM, VMEM), input_output_aliases={8: 0},
         scratch_shapes=[pltpu.VMEM((cells, 16, CELL), BF16), pltpu.VMEM((cells, 16, CELL), BF16),
                         pltpu.VMEM((cells, 8, CELL), F32), pltpu.VMEM((2, 4, 64, CELL), F32)]
         + [pltpu.SMEM((4 * npairs + (10 + STEPS) * U,), jnp.int32)] * 3 + scratch_loop(U),
-        compiler_params=PARAMS, name="remote")(rpos, counts, rcounts, pairs, *tables, L, Q, acc)
+        compiler_params=PARAMS, name="remote")(rpos, counts, rcounts, pairs, *tables, pinned(L), pinned(Q), pinned(acc))
+
+
+def own_call(U, own, half, sizes, tables, L, R, Q, acc):
+    return pl.pallas_call(
+        functools.partial(own_kernel, U, (acc.shape[0] - 1) // 2),
+        out_shape=pltpu.VMEM(acc.shape, F32),
+        in_specs=[SMEM, SMEM, SMEM, VMEM, VMEM, VMEM, VMEM, VMEM],
+        out_specs=VMEM, input_output_aliases={7: 0}, scratch_shapes=scratch_loop(U),
+        compiler_params=PARAMS, name="own")(own, half, sizes, tables[0], pinned(L), pinned(R), pinned(Q), pinned(acc))
 
 
 def final_call(acc, pos, q, occupied, send, back):
@@ -363,7 +421,7 @@
         functools.partial(final_kernel, leaves, remotes, slots),
         out_shape=jax.ShapeDtypeStruct((4, leaves, slots), F32),
         in_specs=[VMEM, VMEM, VMEM, VMEM, SMEM, VMEM], out_specs=VMEM,
-        compiler_params=PARAMS, name="final")(acc, pos, q, occupied, send, back)
+        compiler_params=PARAMS, name="final")(pinned(acc), pos, q, occupied, send, back)
 
 
 def shifted(value, axis, by):
@@ -385,9 +443,10 @@
     outgoing = jnp.take(jnp.concatenate([positions, charges[None]], 0), send_left, axis=1)
     remote = shifted(outgoing, AXES, -1)
     remote_counts = shifted(jnp.take(counts, send_left), AXES, -1)
-    acc, L, Q = local_call(GROUP, positions, charges, counts, pairs, tables, near)
+    acc, L, Q, R, own, half, sizes = local_call(GROUP, positions, charges, counts, pairs, tables, near)
     acc, back = remote_call(GROUP, remote, counts, remote_counts, pairs, tables, L, Q, acc, leaves + near, remotes)
     returned = shifted(back, AXES, 1)
+    acc = own_call(GROUP, own, half, sizes, tables, L, R, Q, acc)
     return final_call(acc, positions, charges, occupied, send_left, returned)
 
 

time: 182 us -> 152 us (0.84)
  waiting for transfers between devices: 16.6 us -> 0.01 us
  Pallas kernels: 138 us -> 125 us
    pallas_call x1, Pallas kernels: 78.2 us -> 31.2 us  [local_call(): pl.pallas_call(functools.partial(local_kernel, U, leaves, slots, npairs),...]
    pallas_call x0 -> x1, Pallas kernels: none -> 43.4 us  [own_call(): pl.pallas_call(functools.partial(own_kernel, U, (acc.shape[0] - 1) // 2),...]
    ppermute x3, waiting for transfers between devices: 16.6 us -> 0.01 us  [shifted(): lax.ppermute(value, axis, [(i, i + by) for i in range(length) if 0 <= i +...]
    pallas_call x1, Pallas kernels: 50.9 us -> 43.8 us  [remote_call(): pl.pallas_call(functools.partial(remote_kernel, U, leaves, remotes, slots...]
    concatenate x1, other arithmetic: 0.95 us -> 3.87 us  [on_device(): jnp.concatenate([positions, charges[None]], 0)]
    pallas_call x1, Pallas kernels: 9.32 us -> 6.56 us  [final_call(): pl.pallas_call(functools.partial(final_kernel, leaves, remotes, slots), o...]
    unnamed x17 -> x15, local copies, waits for them, and re-layouts: 4.45 us -> 2.44 us
  transfers between devices with their start and end apart: 3 -> 3, of which waited for: 1 -> 0; matrix products, arithmetic and copies ran while one was open for 2% -> 0% of each run, Pallas kernels for 43% -> 50%
where the time goes in v3:
time: 152 us; the launch traced here: 150 us
  Pallas kernels  125 us (82%)
  starting transfers between devices  10.9 us (7%)
  local copies, waits for them, and re-layouts  8.01 us (5%)
  other arithmetic  5.74 us (4%)
    pallas_call x1, Pallas kernels, remote_call(): pl.pallas_call(functools.partial(remote_kernel, U, leaves, remotes, slots...  43.8 us
    pallas_call x1, Pallas kernels, own_call(): pl.pallas_call(functools.partial(own_kernel, U, (acc.shape[0] - 1) // 2),...  43.4 us
    pallas_call x1, Pallas kernels, local_call(): pl.pallas_call(functools.partial(local_kernel, U, leaves, slots, npairs),...  31.2 us
    ppermute x3, starting transfers between devices, shifted(): lax.ppermute(value, axis, [(i, i + by) for i in range(length) if 0 <= i +...  10.9 us
    pallas_call x1, Pallas kernels, final_call(): pl.pallas_call(functools.partial(final_kernel, leaves, remotes, slots), o...  6.56 us
    concatenate x1, other arithmetic, on_device(): jnp.concatenate([positions, charges[None]], 0)  3.87 us
  transfers between devices with their start and end apart: 3, of which 0 were waited for; matrix products, arithmetic and copies ran while one was open for 0% of the time, Pallas kernels for 50%

profile of v3, /device:TPU:96, one launch (start us, length us, event | category | flops | bytes accessed | tf_op | source)
XLA Modules:
  0.0 149.9 jit_solution(14326601087586959894)
XLA Ops:
  0.0 0.0 copy-start.1
  0.0 1.3 fusion.3
  1.3 0.5 copy.11
  1.9 0.0 copy-done.1
  1.9 0.0 copy-start.4
  1.9 0.0 copy-start
  1.9 2.4 %copy.10 = f32[3,512,256]{2,0,1:T(4,128)} copy(f32[3,512,256]{2,1,0:T(8,128)S(1)} %copy-done.1) | data formatting | bytes 3145728 | tf_op args[0]
  4.3 0.0 copy-done.4
  4.3 0.0 copy-done
  4.3 1.9 %gather_fusion.1 = s32[256]{0:T(256)S(1)} fusion(s32[512]{0:T(512)S(1)} %copy-done, s32[1024]{0:T(1024)S(1)} %pad_clamp_fusion), kind=kCustom, calls=%fused_computation.1 | custom fusion | bytes 3072 | tf_op jit(solution)/shard_map/jit(_take)/gather | solution.py:445
  6.3 3.9 %pad_maximum_fusion = f32[4,512,256]{2,0,1:T(4,128)} fusion(f32[1,512,256]{2,0,1:T(1,128)S(1)} %copy.11, f32[3,512,256]{2,0,1:T(4,128)} %copy.10), kind=kLoop, calls=%fused_computation.2 | loop fusion | flops 524288 | bytes 4194304 | tf_op jit(solution)/shard_map/concatenate | solution.py:443
  10.1 0.0 copy-start.5
  10.1 2.9 %gather_fusion = f32[256,4,256]{2,1,0:T(4,128)S(1)} fusion(f32[4,512,256]{2,0,1:T(4,128)} %pad_maximum_fusion, s32[1024]{0:T(1024)S(1)} %pad_clamp_fusion), kind=kCustom, calls=%fused_computation | custom fusion | bytes 2098176 | tf_op jit(solution)/shard_map/jit(_take)/gather | solution.py:443
  13.1 0.0 copy-start.6
  13.1 0.0 copy-start.2
  13.1 0.0 copy-start.3
  13.1 0.3 fusion
  13.4 6.4 %collective-permute-start = (f32[4,256,256]{2,1,0:T(8,128)S(1)}, f32[4,256,256]{2,1,0:T(8,128)S(1)}, u32[]{:S(2)}, u32[]{:S(2)}) collective-permute-start(f32[4,256,256]{2,1,0:T(8,128)S(1)} %fusion), channel_id=1, source_target_pairs={{1,0},{2,1},{3,2},{4,3},{5,4},{6,5},{7,6},{8,7},{9,8},{10,9},{11,1... | collective-permute-start | bytes 3145736 | tf_op jit(solution)/shard_map/ppermute | solution.py:429
  19.8 2.6 %collective-permute-start.1 = (s32[256]{0:T(256)S(1)}, s32[256]{0:T(256)S(1)}, u32[]{:S(2)}, u32[]{:S(2)}) collective-permute-start(s32[256]{0:T(256)S(1)} %get-tuple-element.23), channel_id=1, source_target_pairs={{1,0},{2,1},{3,2},{4,3},{5,4},{6,5},{7,6},{8,7},{9,8},{10,9},{11,1... | collective-permute-start | bytes 3080 | tf_op jit(solution)/shard_map/ppermute | solution.py:429
  22.4 0.0 copy-done.5
  22.4 0.1 fusion.2.q
  22.6 0.0 copy-done.6
  22.6 0.2 jit_solution_.3.shift
  22.7 0.0 copy-done.2
  22.8 0.0 copy-done.3
  22.8 31.2 %local.1 = (f32[1025,8,128]{2,1,0:T(8,128)S(1)}, bf16[1025,32,128]{2,1,0:T(8,128)(2,1)S(1)}, bf16[1025,16,128]{2,1,0:T(8,128)(2,1)S(1)}, bf16[1025,16,128]{2,1,0...) custom-call(f32[3,512,256]{2,1,0:T(8,128)S(1)} %copy-done.1, f32[512,256]{1,0:T(8,128)S(1)} %fusion.2.q, ...), custom_call_target="tpu_custom_call" | custom-call | tf_op jit(solution)/shard_map/local/pallas_call | solution.py:380
  54.0 0.0 collective-permute-done.1.rcounts
  54.0 0.0 collective-permute-done.rpos
  54.0 43.8 %remote.1 = (f32[1025,8,128]{2,1,0:T(8,128)S(1)}, f32[4,256,256]{2,1,0:T(8,128)S(1)}) custom-call(f32[4,256,256]{2,1,0:T(8,128)S(1)} %collective-permute-done.rpos, s32[512]{0:T(512)S(1)} %copy-done, s32[256]{0:T(256)S(1)} %collective-permute-done.1.rcounts, s32[3,896]{1,0:T(4,128)S(1)} %copy-done.3, ...), custom_call_target="tpu_custom_call", output_to_operand_aliasing={{0}: (8, {})} | custom-call | tf_op jit(solution)/shard_map/remote/pallas_call | solution.py:397
  97.8 1.9 %collective-permute-start.2 = (f32[4,256,256]{2,1,0:T(8,128)S(1)}, f32[4,256,256]{2,1,0:T(8,128)S(1)}, u32[]{:S(2)}, u32[]{:S(2)}) collective-permute-start(f32[4,256,256]{2,1,0:T(8,128)S(1)} %get-tuple-element.22), channel_id=1, source_target_pairs={{0,1},{1,2},{2,3},{3,4},{4,5},{5,6},{6,7},{7,8},{8,9},{9,10},{10,1... | collective-permute-start | bytes 3145736 | tf_op jit(solution)/shard_map/ppermute | solution.py:429
  99.7 0.1 fusion.1.occupied
  99.8 43.4 %own.1.acc = f32[1025,8,128]{2,1,0:T(8,128)S(1)} custom-call(s32[1136]{0:T(1024)S(1)} %get-tuple-element.14.own, s32[624]{0:T(1024)S(1)} %get-tuple-element.15.half, s32[2]{0:T(128)S(1)} %get-tuple-element.16.sizes, bf16[27,32,128]{2,1,0:T(8,128)(2,1)S(1)} %copy-done.2, ...), custom_call_target="tpu_custom_call", output_to_operand_aliasing={{}: (7, {})} | custom-call | tf_op jit(solution)/shard_map/own/pallas_call | solution.py:409
  143.3 0.0 collective-permute-done.2.back
  143.3 6.6 %final.1 = f32[4,512,256]{2,1,0:T(8,128)} custom-call(f32[1025,8,128]{2,1,0:T(8,128)S(1)} %own.1.acc, f32[3,512,256]{2,1,0:T(8,128)S(1)} %copy-done.1, f32[512,256]{1,0:T(8,128)S(1)} %fusion.2.q, f32[512,256]{1,0:T(8,128)S(1)} %fusion.1.occupied, s32[256]{0:T(256)S(1)} %copy-done.4, f32[4,256,256]{2,1,0:T(8,128)S(1)} %collective-permute-done.2.back), custom_call_target="tpu_custom_call" | custom-call | tf_op jit(solution)/shard_map/final/pallas_call | solution.py:420
  (3 shorter events, 0.0 us)
Async XLA Ops:
  0.0 1.9 %copy-start.1 = (f32[3,512,256]{2,1,0:T(8,128)S(1)}, f32[3,512,256]{2,1,0:T(8,128)}, u32[]{:S(2)}) copy-start(f32[3,512,256]{2,1,0:T(8,128)} %pos.3) | copy-start | bytes 4718596
  1.9 2.4 %copy-start.4 = (s32[256]{0:T(256)S(1)}, s32[256]{0:T(256)}, u32[]{:S(2)}) copy-start(s32[256]{0:T(256)} %send.1) | copy-start | bytes 3076
  1.9 2.4 %copy-start = (s32[512]{0:T(512)S(1)}, s32[512]{0:T(512)}, u32[]{:S(2)}) copy-start(s32[512]{0:T(512)} %counts.3) | copy-start | bytes 6148
  10.1 12.3 %copy-start.5 = (f32[512,256]{1,0:T(8,128)S(1)}, f32[512,256]{1,0:T(8,128)}, u32[]{:S(2)}) copy-start(f32[512,256]{1,0:T(8,128)} %param.8) | copy-start | bytes 1572868
  13.1 9.5 %copy-start.6 = (f32[27,32]{1,0:T(8,128)S(1)}, f32[27,32]{1,0:T(8,128)}, u32[]{:S(2)}) copy-start(f32[27,32]{1,0:T(8,128)} %constant.36.clone) | copy-start | bytes 10372
  13.1 9.7 %copy-start.2 = (bf16[27,32,128]{2,1,0:T(8,128)(2,1)S(1)}, bf16[27,32,128]{2,1,0:T(8,128)(2,1)}, u32[]{:S(2)}) copy-start(bf16[27,32,128]{2,1,0:T(8,128)(2,1)} %constant.35.clone.table) | copy-start | bytes 663556
  13.1 9.7 %copy-start.3 = (s32[3,896]{1,0:T(4,128)S(1)}, s32[3,896]{1,0:T(4,128)}, u32[]{:S(2)}) copy-start(s32[3,896]{1,0:T(4,128)} %pairs.3) | copy-start | bytes 32260
  13.4 40.6 %collective-permute-start = (f32[4,256,256]{2,1,0:T(8,128)S(1)}, f32[4,256,256]{2,1,0:T(8,128)S(1)}, u32[]{:S(2)}, u32[]{:S(2)}) collective-permute-start(f32[4,256,256]{2,1,0:T(8,128)S(1)} %fusion), channel_id=1, source_target_pairs={{1,0},{2,1},{3,2},{4,3},{5,4},{6,5},{7,6},{8,7},{9,8},{10,9},{11,1... | collective-permute-start | bytes 3145736 | tf_op jit(solution)/shard_map/ppermute | solution.py:429
  19.8 34.2 %collective-permute-start.1 = (s32[256]{0:T(256)S(1)}, s32[256]{0:T(256)S(1)}, u32[]{:S(2)}, u32[]{:S(2)}) collective-permute-start(s32[256]{0:T(256)S(1)} %get-tuple-element.23), channel_id=1, source_target_pairs={{1,0},{2,1},{3,2},{4,3},{5,4},{6,5},{7,6},{8,7},{9,8},{10,9},{11,1... | collective-permute-start | bytes 3080 | tf_op jit(solution)/shard_map/ppermute | solution.py:429
  97.8 45.5 %collective-permute-start.2 = (f32[4,256,256]{2,1,0:T(8,128)S(1)}, f32[4,256,256]{2,1,0:T(8,128)S(1)}, u32[]{:S(2)}, u32[]{:S(2)}) collective-permute-start(f32[4,256,256]{2,1,0:T(8,128)S(1)} %get-tuple-element.22), channel_id=1, source_target_pairs={{0,1},{1,2},{2,3},{3,4},{4,5},{5,6},{6,7},{7,8},{8,9},{9,10},{10,1... | collective-permute-start | bytes 3145736 | tf_op jit(solution)/shard_map/ppermute | solution.py:429

commit v4 on v3

--- a/solution.py
+++ b/solution.py
@@ -11,6 +11,9 @@
 SOFTEN = 0.05
 CELL = 128
 STEPS = 4
+UNROLL = 2
+DIRECT = (7,)
+NT = (((1,), (1,)), ((), ()))
 NN = (((1,), (0,)), ((), ()))
 TN = (((0,), (0,)), ((), ()))
 
@@ -116,7 +119,7 @@
                     L[to] = jnp.concatenate([first_half, second, third, fourth], 0).astype(BF16)
         return carry
 
-    return lax.fori_loop(0, leaves // 8, body, carry)
+    return lax.fori_loop(0, leaves // 8, body, carry, unroll=UNROLL)
 
 
 def finish_list(lists, n, U, values):
@@ -126,23 +129,30 @@
             r[n + i] = v
 
 
-def pipeline(U, batches, aim, gram_operands, aimed, gram, weights, turned, last, middle):
+def pipeline(U, batches, aim, gram_operands, aimed, gram, weights, turned, wide, last, middle):
     def step(j):
         if last is not None:
             for k in range(U):
-                last(j * U + k, turned[k])
+                if k not in DIRECT:
+                    last(j * U + k, turned[k], NN)
         for k in range(U):
             w = weights[k]
             middle((j + 1) * U + k, w)
-            if last is not None:
+            if last is not None and k in DIRECT:
+                last((j + 1) * U + k, wide[k], NT)
+            elif last is not None:
                 turned[k, 0:CELL] = w[0:CELL].T
                 turned[k, CELL:] = w[CELL:].T
         for k in range(U):
             w = lax.rsqrt(gram[k])
             w3 = w * w * w
             high = w3.astype(BF16)
+            low = (w3 - high.astype(F32)).astype(BF16)
             weights[k, 0:CELL] = high
-            weights[k, CELL:] = (w3 - high.astype(F32)).astype(BF16)
+            weights[k, CELL:] = low
+            if last is not None and k in DIRECT:
+                wide[k, :, 0:CELL] = high
+                wide[k, :, CELL:] = low
         for k in range(U):
             gram[k] = lax.dot_general(aimed[k], gram_operands((j + 3) * U + k), NN, preferred_element_type=F32)
         for k in range(U):
@@ -154,8 +164,8 @@
             step(i * STEPS + s)
 
 
-def summed(q, w):
-    out = lax.dot_general(jnp.concatenate([q, q], 1), w, NN, preferred_element_type=F32)
+def summed(q, w, form=NN):
+    out = lax.dot_general(jnp.concatenate([q, q], 1), w, form, preferred_element_type=F32)
     return out[0:8] + out[8:16]
 
 
@@ -175,8 +185,8 @@
     def on_source(i, w):
         acc_b[lb[i]] += moved(summed(Qa[la[i]], w), shift, lc[i], 16)
 
-    def on_target(i, w):
-        acc_a[la[i]] += moved(summed(Qb[lb[i]], w), shift, lc[i], 0)
+    def on_target(i, w, form):
+        acc_a[la[i]] += moved(summed(Qb[lb[i]], w, form), shift, lc[i], 0)
 
     pipeline(U, lax.div(n - 4 * U + U - 1, U), lambda i: L[la[i]], operands, *scratch, on_target, on_source)
 
@@ -191,8 +201,8 @@
     def on_source(i, w):
         acc[second(i)] += summed(Q[cells[i]], w)
 
-    def on_target(i, w):
-        acc[cells[i]] += summed(Q[second(i)], w)
+    def on_target(i, w, form):
+        acc[cells[i]] += summed(Q[second(i)], w, form)
 
     pipeline(U, lax.div(n - 4 * U + U - 1, U), lambda i: L[cells[i]], operands, *scratch, on_target, on_source)
 
@@ -207,11 +217,12 @@
     pipeline(U, lax.div(n - 4 * U + U - 1, U), lambda i: L[cells[i]], operands, *scratch, None, on_target)
 
 
-def clear(aimed, gram, weights, turned):
+def clear(aimed, gram, weights, turned, wide):
     aimed[...] = jnp.zeros_like(aimed)
     gram[...] = jnp.ones_like(gram)
     weights[...] = jnp.zeros_like(weights)
     turned[...] = jnp.zeros_like(turned)
+    wide[...] = jnp.zeros_like(wide)
 
 
 def start_list(lists, U, values):
@@ -366,7 +377,30 @@
 
 
 def scratch_loop(U):
-    return [pltpu.VMEM((U, CELL, 32), BF16), pltpu.VMEM((U, CELL, CELL), F32)] + [pltpu.VMEM((U, 2 * CELL, CELL), BF16)] * 2
+    return [pltpu.VMEM((U, CELL, 32), BF16), pltpu.VMEM((U, CELL, CELL), F32)] + [pltpu.VMEM((U, 2 * CELL, CELL), BF16)] * 2 + [pltpu.VMEM((U, CELL, 2 * CELL), BF16)]
+
+
+def gather_kernel(remotes, pos, q, counts, send, out):
+    lane = lax.broadcasted_iota(jnp.int32, (1, q.shape[1]), 1)
+
+    def body(g, _):
+        for k in range(8):
+            to, at = pl.ds(8 * g + k, 1), send[8 * g + k]
+            row, here = pl.ds(at, 1), lane < counts[at]
+            out[0, to, :] = jnp.where(here, pos[0, row, :], 2.0)
+            out[1, to, :] = pos[1, row, :]
+            out[2, to, :] = pos[2, row, :]
+            out[3, to, :] = jnp.where(here, q[row, :], 0.0)
+        return 0
+
+    lax.fori_loop(0, remotes // 8, body, 0)
+
+
+def gather_call(pos, q, counts, send):
+    return pl.pallas_call(
+        functools.partial(gather_kernel, send.shape[0]),
+        out_shape=jax.ShapeDtypeStruct((4, send.shape[0], q.shape[1]), F32),
+        in_specs=[VMEM, VMEM, SMEM, SMEM], out_specs=VMEM, compiler_params=PARAMS, name="gather")(pos, q, counts, send)
 
 
 def pinned(x):
@@ -437,12 +471,12 @@
     leaves, slots = charges.shape
     remotes = send_left.shape[0]
     near = pairs.shape[1] - leaves - remotes
+    remote = shifted(gather_call(positions, charges, counts, send_left), AXES, -1)
     occupied = (jnp.arange(slots)[None, :] < counts[:, None]).astype(jnp.float32)
     charges = charges * occupied
     tables = offset_tables()
-    outgoing = jnp.take(jnp.concatenate([positions, charges[None]], 0), send_left, axis=1)
-    remote = shifted(outgoing, AXES, -1)
-    remote_counts = shifted(jnp.take(counts, send_left), AXES, -1)
+    empty = (remote[0, :, CELL] > 1.5) | (lax.axis_index(AXES) == lax.axis_size(AXES) - 1)
+    remote_counts = jnp.where(empty, 0, slots).astype(jnp.int32)
     acc, L, Q, R, own, half, sizes = local_call(GROUP, positions, charges, counts, pairs, tables, near)
     acc, back = remote_call(GROUP, remote, counts, remote_counts, pairs, tables, L, Q, acc, leaves + near, remotes)
     returned = shifted(back, AXES, 1)

time: 152 us -> 141 us (0.928); the launches traced: 150 us -> 140 us
  other arithmetic: 5.74 us -> 1.43 us
  local copies, waits for them, and re-layouts: 8.01 us -> 4 us
  starting transfers between devices: 10.9 us -> 8.3 us
    gather x2 -> x0, local copies, waits for them, and re-layouts: 4.87 us -> none  [the longest x1 2.92 us: on_device(): jnp.take(jnp.concatenate([positions, charges[None]], 0), send_left, axis=1)]
    concatenate x1 -> x0, other arithmetic: 3.87 us -> none  [on_device(): jnp.concatenate([positions, charges[None]], 0)]
    pallas_call x0 -> x1, Pallas kernels: none -> 2.95 us  [gather_call(): pl.pallas_call(functools.partial(gather_kernel, send.shape[0]), out_shape...]
    ppermute x3 -> x2, starting transfers between devices: 10.9 us -> 8.3 us  [shifted(): lax.ppermute(value, axis, [(i, i + by) for i in range(length) if 0 <= i +...]
    pallas_call x1, Pallas kernels: 31.2 us -> 29.6 us  [local_call(): pl.pallas_call(functools.partial(local_kernel, U, leaves, slots, npairs),...]
    pallas_call x1, Pallas kernels: 43.4 us -> 45 us  [own_call(): pl.pallas_call(functools.partial(own_kernel, U, (acc.shape[0] - 1) // 2),...]
    unnamed x15 -> x20, local copies, waits for them, and re-layouts: 2.44 us -> 3.83 us
  transfers between devices with their start and end apart: 3 -> 2, of which waited for: 0 -> 0; matrix products, arithmetic and copies ran while one was open for 0% -> 1% of each run, Pallas kernels for 50% -> 53%
where the time goes in v4:
time: 141 us; the launch traced here: 140 us
  Pallas kernels  126 us (89%)
  starting transfers between devices  8.3 us (6%)
  local copies, waits for them, and re-layouts  4 us (3%)
  other arithmetic  1.43 us (1%)
    pallas_call x1, Pallas kernels, own_call(): pl.pallas_call(functools.partial(own_kernel, U, (acc.shape[0] - 1) // 2),...  45 us
    pallas_call x1, Pallas kernels, remote_call(): pl.pallas_call(functools.partial(remote_kernel, U, leaves, remotes, slots...  42.3 us
    pallas_call x1, Pallas kernels, local_call(): pl.pallas_call(functools.partial(local_kernel, U, leaves, slots, npairs),...  29.6 us
    ppermute x2, starting transfers between devices, shifted(): lax.ppermute(value, axis, [(i, i + by) for i in range(length) if 0 <= i +...  8.3 us
    pallas_call x1, Pallas kernels, final_call(): pl.pallas_call(functools.partial(final_kernel, leaves, remotes, slots), o...  6.56 us
    unnamed x20, local copies, waits for them, and re-layouts  3.83 us
    pallas_call x1, Pallas kernels, gather_call(): pl.pallas_call(functools.partial(gather_kernel, send.shape[0]), out_shape...  2.95 us
  transfers between devices with their start and end apart: 2, of which 0 were waited for; matrix products, arithmetic and copies ran while one was open for 1% of the time, Pallas kernels for 53%

profile of v4, /device:TPU:96, one launch (start us, length us, event | category | flops | bytes accessed | tf_op | source)
XLA Modules:
  0.0 140.4 jit_solution(5716680628071548194)
XLA Ops:
  0.0 0.0 copy-start
  0.0 1.4 %copy-done = f32[3,512,256]{2,1,0:T(8,128)S(1)} copy-done((f32[3,512,256]{2,1,0:T(8,128)S(1)}, f32[3,512,256]{2,1,0:T(8,128)}, u32[]{:S(2)}) %copy-start) | copy-done | bytes 1572888
  1.4 0.0 copy-start.2
  1.4 1.0 copy-done.2
  2.5 0.0 copy-start.5
  2.5 0.7 copy-done.5
  3.1 0.0 copy-start.7
  3.1 0.7 copy-done.7
  3.8 0.0 copy-start.9
  3.8 0.0 copy-start.1
  3.8 0.0 copy-start.3
  3.8 0.0 copy-start.4
  3.8 0.0 copy-start.6
  3.8 2.9 %gather.1 = f32[4,256,256]{2,1,0:T(8,128)} custom-call(f32[3,512,256]{2,1,0:T(8,128)S(1)} %copy-done, f32[512,256]{1,0:T(8,128)S(1)} %copy-done.2, s32[512]{0:T(512)S(1)} %copy-done.5, s32[256]{0:T(256)S(1)} %copy-done.7), custom_call_target="tpu_custom_call" | custom-call | tf_op jit(solution)/shard_map/gather/pallas_call | solution.py:400
  6.8 6.4 %collective-permute-start = (f32[4,256,256]{2,1,0:T(8,128)}, f32[4,256,256]{2,1,0:T(8,128)S(1)}, u32[]{:S(2)}, u32[]{:S(2)}) collective-permute-start(f32[4,256,256]{2,1,0:T(8,128)} %gather.1), channel_id=1, source_target_pairs={{1,0},{2,1},{3,2},{4,3},{5,4},{6,5},{7,6},{8,7},{9,8},{10,9},{11,1... | collective-permute-start | bytes 3145736 | tf_op jit(solution)/shard_map/ppermute | solution.py:463
  13.2 1.2 fusion.1.q
  14.4 0.0 copy-done.9
  14.4 0.2 jit_solution_.3.shift
  14.6 0.0 copy-done.1
  14.6 0.0 copy-done.3
  14.6 0.0 copy-done.4
  14.6 0.0 copy-done.6
  14.6 29.6 %local.1 = (f32[1025,8,128]{2,1,0:T(8,128)S(1)}, bf16[1025,32,128]{2,1,0:T(8,128)(2,1)S(1)}, bf16[1025,16,128]{2,1,0:T(8,128)(2,1)S(1)}, bf16[1025,16,128]{2,1,0...) custom-call(f32[3,512,256]{2,1,0:T(8,128)S(1)} %copy-done.1, f32[512,256]{1,0:T(8,128)S(1)} %fusion.1.q, ...), custom_call_target="tpu_custom_call" | custom-call | tf_op jit(solution)/shard_map/local/pallas_call | solution.py:414
  44.2 0.0 collective-permute-done.rpos
  44.2 0.1 select_reduce_fusion.rcounts
  44.3 42.3 %remote.1 = (f32[1025,8,128]{2,1,0:T(8,128)S(1)}, f32[4,256,256]{2,1,0:T(8,128)S(1)}) custom-call(f32[4,256,256]{2,1,0:T(8,128)S(1)} %collective-permute-done.rpos, s32[512]{0:T(512)S(1)} %copy-done.6, s32[256]{0:T(256)S(1)} %select_reduce_fusion.rcounts, s32[3,896]{1,0:T(4,128)S(1)} %copy-done.4, ...), custom_call_target="tpu_custom_call", output_to_operand_aliasing={{0}: (8, {})} | custom-call | tf_op jit(solution)/shard_map/remote/pallas_call | solution.py:431
  86.7 1.9 %collective-permute-start.1 = (f32[4,256,256]{2,1,0:T(8,128)S(1)}, f32[4,256,256]{2,1,0:T(8,128)S(1)}, u32[]{:S(2)}, u32[]{:S(2)}) collective-permute-start(f32[4,256,256]{2,1,0:T(8,128)S(1)} %get-tuple-element.22), channel_id=1, source_target_pairs={{0,1},{1,2},{2,3},{3,4},{4,5},{5,6},{6,7},{7,8},{8,9},{9,10},{10,1... | collective-permute-start | bytes 3145736 | tf_op jit(solution)/shard_map/ppermute | solution.py:463
  88.6 0.1 fusion.occupied
  88.8 0.0 copy-start.8
  88.8 45.0 %own.1.acc = f32[1025,8,128]{2,1,0:T(8,128)S(1)} custom-call(s32[1136]{0:T(1024)S(1)} %get-tuple-element.14.own, s32[624]{0:T(1024)S(1)} %get-tuple-element.15.half, s32[2]{0:T(128)S(1)} %get-tuple-element.16.sizes, bf16[27,32,128]{2,1,0:T(8,128)(2,1)S(1)} %copy-done.3, ...), custom_call_target="tpu_custom_call", output_to_operand_aliasing={{}: (7, {})} | custom-call | tf_op jit(solution)/shard_map/own/pallas_call | solution.py:443
  133.8 0.0 collective-permute-done.1.back
  133.8 0.0 copy-done.8
  133.8 6.6 %final.1 = f32[4,512,256]{2,1,0:T(8,128)} custom-call(f32[1025,8,128]{2,1,0:T(8,128)S(1)} %own.1.acc, f32[3,512,256]{2,1,0:T(8,128)S(1)} %copy-done.1, f32[512,256]{1,0:T(8,128)S(1)} %fusion.1.q, f32[512,256]{1,0:T(8,128)S(1)} %fusion.occupied, s32[256]{0:T(256)S(1)} %copy-done.8, f32[4,256,256]{2,1,0:T(8,128)S(1)} %collective-permute-done.1.back), custom_call_target="tpu_custom_call" | custom-call | tf_op jit(solution)/shard_map/final/pallas_call | solution.py:454
Async XLA Ops:
  0.0 1.4 %copy-start = (f32[3,512,256]{2,1,0:T(8,128)S(1)}, f32[3,512,256]{2,1,0:T(8,128)}, u32[]{:S(2)}) copy-start(f32[3,512,256]{2,1,0:T(8,128)} %pos.5) | copy-start | bytes 4718596
  1.4 1.0 copy-start.2
  2.5 0.7 copy-start.5
  3.1 0.7 copy-start.7
  3.8 10.6 %copy-start.9 = (f32[27,32]{1,0:T(8,128)S(1)}, f32[27,32]{1,0:T(8,128)}, u32[]{:S(2)}) copy-start(f32[27,32]{1,0:T(8,128)} %constant.25.clone) | copy-start | bytes 10372
  3.8 10.7 %copy-start.1 = (f32[3,512,256]{2,1,0:T(8,128)S(1)}, f32[3,512,256]{2,1,0:T(8,128)}, u32[]{:S(2)}) copy-start(f32[3,512,256]{2,1,0:T(8,128)} %pos.5) | copy-start | bytes 4718596
  3.8 10.7 %copy-start.3 = (bf16[27,32,128]{2,1,0:T(8,128)(2,1)S(1)}, bf16[27,32,128]{2,1,0:T(8,128)(2,1)}, u32[]{:S(2)}) copy-start(bf16[27,32,128]{2,1,0:T(8,128)(2,1)} %constant.24.clone.table) | copy-start | bytes 663556
  3.8 10.8 %copy-start.4 = (s32[3,896]{1,0:T(4,128)S(1)}, s32[3,896]{1,0:T(4,128)}, u32[]{:S(2)}) copy-start(s32[3,896]{1,0:T(4,128)} %pairs.3) | copy-start | bytes 32260
  3.8 10.8 %copy-start.6 = (s32[512]{0:T(512)S(1)}, s32[512]{0:T(512)}, u32[]{:S(2)}) copy-start(s32[512]{0:T(512)} %counts.5) | copy-start | bytes 6148
  6.8 37.4 %collective-permute-start = (f32[4,256,256]{2,1,0:T(8,128)}, f32[4,256,256]{2,1,0:T(8,128)S(1)}, u32[]{:S(2)}, u32[]{:S(2)}) collective-permute-start(f32[4,256,256]{2,1,0:T(8,128)} %gather.1), channel_id=1, source_target_pairs={{1,0},{2,1},{3,2},{4,3},{5,4},{6,5},{7,6},{8,7},{9,8},{10,9},{11,1... | collective-permute-start | bytes 3145736 | tf_op jit(solution)/shard_map/ppermute | solution.py:463
  86.7 47.1 %collective-permute-start.1 = (f32[4,256,256]{2,1,0:T(8,128)S(1)}, f32[4,256,256]{2,1,0:T(8,128)S(1)}, u32[]{:S(2)}, u32[]{:S(2)}) collective-permute-start(f32[4,256,256]{2,1,0:T(8,128)S(1)} %get-tuple-element.22), channel_id=1, source_target_pairs={{0,1},{1,2},{2,3},{3,4},{4,5},{5,6},{6,7},{7,8},{8,9},{9,10},{10,1... | collective-permute-start | bytes 3145736 | tf_op jit(solution)/shard_map/ppermute | solution.py:463
  88.8 45.0 %copy-start.8 = (s32[256]{0:T(256)S(1)}, s32[256]{0:T(256)}, u32[]{:S(2)}) copy-start(s32[256]{0:T(256)} %send.3) | copy-start | bytes 3076

commit v5 on v4

--- a/solution.py
+++ b/solution.py
@@ -10,9 +10,7 @@
 BF16 = jnp.bfloat16
 SOFTEN = 0.05
 CELL = 128
-STEPS = 4
 UNROLL = 2
-DIRECT = (7,)
 NT = (((1,), (1,)), ((), ()))
 NN = (((1,), (0,)), ((), ()))
 TN = (((0,), (0,)), ((), ()))
@@ -123,7 +121,7 @@
 
 
 def finish_list(lists, n, U, values):
-    @pl.loop(0, (5 + STEPS) * U)
+    @pl.loop(0, (5 + U) * U)
     def _(i):
         for r, v in zip(lists, values):
             r[n + i] = v
@@ -133,12 +131,12 @@
     def step(j):
         if last is not None:
             for k in range(U):
-                if k not in DIRECT:
+                if k < U - 1:
                     last(j * U + k, turned[k], NN)
         for k in range(U):
             w = weights[k]
             middle((j + 1) * U + k, w)
-            if last is not None and k in DIRECT:
+            if last is not None and k == U - 1:
                 last((j + 1) * U + k, wide[k], NT)
             elif last is not None:
                 turned[k, 0:CELL] = w[0:CELL].T
@@ -150,7 +148,7 @@
             low = (w3 - high.astype(F32)).astype(BF16)
             weights[k, 0:CELL] = high
             weights[k, CELL:] = low
-            if last is not None and k in DIRECT:
+            if last is not None and k == U - 1:
                 wide[k, :, 0:CELL] = high
                 wide[k, :, CELL:] = low
         for k in range(U):
@@ -158,10 +156,10 @@
         for k in range(U):
             aimed[k] = aim((j + 4) * U + k).T
 
-    @pl.loop(0, lax.div(batches + 3 + STEPS, STEPS))
+    @pl.loop(0, lax.div(batches + 3 + U, U))
     def _(i):
-        for s in range(STEPS):
-            step(i * STEPS + s)
+        for s in range(U):
+            step(i * U + s)
 
 
 def summed(q, w, form=NN):
@@ -251,14 +249,14 @@
     Q[at_r] = jnp.zeros(Q.shape[1:], BF16)
 
 
-def local_kernel(U, leaves, slots, npairs, pos, q, counts, pairs, table, shift, acc, L, Q, R, own, half, sizes, stage, la, lb,
+def local_kernel(U, V, leaves, slots, npairs, pos, q, counts, pairs, table, shift, acc, L, Q, R, own, half, sizes, stage, la, lb,
                  lc, *scratch):
     dummy = 2 * leaves
     lists = (la, lb, lc)
     acc[...] = jnp.zeros_like(acc)
     idle_cell(L, R, Q, dummy, dummy)
     clear(*scratch)
-    start_list((own, half), U, (dummy, dummy))
+    start_list((own, half), V, (dummy, dummy))
     start_list(lists, U, (dummy, dummy, 13))
     groups = leaves // 8
     share = npairs // groups
@@ -278,11 +276,11 @@
         return n, nh, nx
 
     n, nh, nx = prepare(lambda i, r, s: pos[i, r, s], lambda r, s: q[r, s], leaves, slots, stage, R, Q, L, extra,
-                        (4 * U, 4 * U, 4 * U))
+                        (4 * V, 4 * V, 4 * U))
     nx = lax.fori_loop(leaves + groups * share, leaves + npairs, lambda i, nx: list_pair(
         lists, nx, pairs, i, 0, counts, counts, leaves, leaves), nx)
-    finish_list((own,), n, U, (dummy,))
-    finish_list((half,), nh, U, (dummy,))
+    finish_list((own,), n, V, (dummy,))
+    finish_list((half,), nh, V, (dummy,))
     finish_list(lists, nx, U, (dummy, dummy, 13))
     sizes[0] = n
     sizes[1] = nh
@@ -349,26 +347,24 @@
             cells = pl.ds(pl.multiple_of(h * leaves + g * 8, 8), 8)
             values = finished(acc, cells, [pos[i, r, lanes] for i in range(3)])
             values[0] = values[0] - q[r, lanes] * (1.0 / np.sqrt(SOFTEN))
+            keep = occupied[r, lanes]
             for i in range(4):
-                out[i, r, lanes] = values[i]
-
-    if send is not None:
-        def give(g, _):
-            rows = [pl.ds(send[8 * g + k], 1) for k in range(8)]
-            r = pl.ds(pl.multiple_of(g * 8, 8), 8)
-            for i in range(4):
-                extra = back[i, r, :]
-                sums = [out[i, rows[k], :] + extra[k : k + 1] for k in range(8)]
-                for k in range(8):
-                    out[i, rows[k], :] = sums[k]
-            return 0
-        lax.fori_loop(0, remotes // 8, give, 0)
-
-    @pl.loop(0, leaves // 8)
-    def _(g):
+                out[i, r, lanes] = values[i] * keep
+
+    def give(g, _):
+        rows = [pl.ds(send[8 * g + k], 1) for k in range(8)]
+        keep = [occupied[row, :] for row in rows]
         r = pl.ds(pl.multiple_of(g * 8, 8), 8)
+        sums = []
         for i in range(4):
-            out[i, r, :] = out[i, r, :] * occupied[r, :]
+            extra = back[i, r, :]
+            sums.append([out[i, rows[k], :] + extra[k : k + 1] * keep[k] for k in range(8)])
+        for i in range(4):
+            for k in range(8):
+                out[i, rows[k], :] = sums[i][k]
+        return 0
+
+    lax.fori_loop(0, remotes // 8, give, 0)
 
 
 SMEM = pl.BlockSpec(memory_space=pltpu.SMEM)
@@ -407,15 +403,15 @@
     return pltpu.with_memory_space_constraint(x, pltpu.VMEM)
 
 
-def local_call(U, pos, q, counts, pairs, tables, npairs):
+def local_call(U, V, pos, q, counts, pairs, tables, npairs):
     leaves, slots = q.shape
     cells = 2 * leaves + 1
-    room = (10 + STEPS) * U
+    room, own_room = (10 + U) * U, (10 + V) * V
     return pl.pallas_call(
-        functools.partial(local_kernel, U, leaves, slots, npairs),
+        functools.partial(local_kernel, U, V, leaves, slots, npairs),
         out_shape=(pltpu.VMEM((cells, 8, CELL), F32), pltpu.VMEM((cells, 32, CELL), BF16),
                    pltpu.VMEM((cells, 16, CELL), BF16), pltpu.VMEM((cells, 16, CELL), BF16),
-                   jax.ShapeDtypeStruct((2 * leaves + room,), jnp.int32), jax.ShapeDtypeStruct((leaves + room,), jnp.int32),
+                   jax.ShapeDtypeStruct((2 * leaves + own_room,), jnp.int32), jax.ShapeDtypeStruct((leaves + own_room,), jnp.int32),
                    jax.ShapeDtypeStruct((2,), jnp.int32)),
         in_specs=[VMEM, VMEM, SMEM, SMEM, VMEM, VMEM],
         out_specs=(VMEM, VMEM, VMEM, VMEM, SMEM, SMEM, SMEM),
@@ -435,7 +431,7 @@
         out_specs=(VMEM, VMEM), input_output_aliases={8: 0},
         scratch_shapes=[pltpu.VMEM((cells, 16, CELL), BF16), pltpu.VMEM((cells, 16, CELL), BF16),
                         pltpu.VMEM((cells, 8, CELL), F32), pltpu.VMEM((2, 4, 64, CELL), F32)]
-        + [pltpu.SMEM((4 * npairs + (10 + STEPS) * U,), jnp.int32)] * 3 + scratch_loop(U),
+        + [pltpu.SMEM((4 * npairs + (10 + U) * U,), jnp.int32)] * 3 + scratch_loop(U),
         compiler_params=PARAMS, name="remote")(rpos, counts, rcounts, pairs, *tables, pinned(L), pinned(Q), pinned(acc))
 
 
@@ -464,7 +460,7 @@
 
 
 AXES = ("leaf", "grp")
-GROUP = 8
+GROUP, OWN_GROUP = 6, 8
 
 
 def on_device(positions, charges, counts, send_left, pairs):
@@ -477,10 +473,10 @@
     tables = offset_tables()
     empty = (remote[0, :, CELL] > 1.5) | (lax.axis_index(AXES) == lax.axis_size(AXES) - 1)
     remote_counts = jnp.where(empty, 0, slots).astype(jnp.int32)
-    acc, L, Q, R, own, half, sizes = local_call(GROUP, positions, charges, counts, pairs, tables, near)
+    acc, L, Q, R, own, half, sizes = local_call(GROUP, OWN_GROUP, positions, charges, counts, pairs, tables, near)
     acc, back = remote_call(GROUP, remote, counts, remote_counts, pairs, tables, L, Q, acc, leaves + near, remotes)
     returned = shifted(back, AXES, 1)
-    acc = own_call(GROUP, own, half, sizes, tables, L, R, Q, acc)
+    acc = own_call(OWN_GROUP, own, half, sizes, tables, L, R, Q, acc)
     return final_call(acc, positions, charges, occupied, send_left, returned)
 
 

time: 141 us -> 136 us (0.965)
  the two profiles are of different devices: /device:TPU:96 before, /device:TPU:95 now
where the time goes in v5:
time: 136 us; the launch traced here: 135 us
  Pallas kernels  120 us (88%)
  starting transfers between devices  9.77 us (7%)
  local copies, waits for them, and re-layouts  4 us (3%)
  other arithmetic  1.43 us (1%)
    pallas_call x1, Pallas kernels, own_call(): pl.pallas_call(functools.partial(own_kernel, U, (acc.shape[0] - 1) // 2),...  43.4 us
    pallas_call x1, Pallas kernels, remote_call(): pl.pallas_call(functools.partial(remote_kernel, U, leaves, remotes, slots...  38.6 us
    pallas_call x1, Pallas kernels, local_call(): pl.pallas_call(functools.partial(local_kernel, U, V, leaves, slots, npair...  28.4 us
    ppermute x2, starting transfers between devices, shifted(): lax.ppermute(value, axis, [(i, i + by) for i in range(length) if 0 <= i +...  9.77 us
    pallas_call x1, Pallas kernels, final_call(): pl.pallas_call(functools.partial(final_kernel, leaves, remotes, slots), o...  6.56 us
    unnamed x20, local copies, waits for them, and re-layouts  3.83 us
    pallas_call x1, Pallas kernels, gather_call(): pl.pallas_call(functools.partial(gather_kernel, send.shape[0]), out_shape...  2.95 us
  transfers between devices with their start and end apart: 2, of which 0 were waited for; matrix products, arithmetic and copies ran while one was open for 1% of the time, Pallas kernels for 53%

profile of v5, /device:TPU:95, one launch (start us, length us, event | category | flops | bytes accessed | tf_op | source)
XLA Modules:
  0.0 135.2 jit_solution(16182475530049119497)
XLA Ops:
  0.0 0.0 copy-start
  0.0 1.4 %copy-done = f32[3,512,256]{2,1,0:T(8,128)S(1)} copy-done((f32[3,512,256]{2,1,0:T(8,128)S(1)}, f32[3,512,256]{2,1,0:T(8,128)}, u32[]{:S(2)}) %copy-start) | copy-done | bytes 1572888
  1.4 0.0 copy-start.2
  1.4 1.0 copy-done.2
  2.5 0.0 copy-start.5
  2.5 0.7 copy-done.5
  3.1 0.0 copy-start.7
  3.1 0.7 copy-done.7
  3.8 0.0 copy-start.9
  3.8 0.0 copy-start.1
  3.8 0.0 copy-start.3
  3.8 0.0 copy-start.4
  3.8 0.0 copy-start.6
  3.8 2.9 %gather.1 = f32[4,256,256]{2,1,0:T(8,128)} custom-call(f32[3,512,256]{2,1,0:T(8,128)S(1)} %copy-done, f32[512,256]{1,0:T(8,128)S(1)} %copy-done.2, s32[512]{0:T(512)S(1)} %copy-done.5, s32[256]{0:T(256)S(1)} %copy-done.7), custom_call_target="tpu_custom_call" | custom-call | tf_op jit(solution)/shard_map/gather/pallas_call | solution.py:396
  6.8 2.6 %collective-permute-start = (f32[4,256,256]{2,1,0:T(8,128)}, f32[4,256,256]{2,1,0:T(8,128)S(1)}, u32[]{:S(2)}, u32[]{:S(2)}) collective-permute-start(f32[4,256,256]{2,1,0:T(8,128)} %gather.1), channel_id=1, source_target_pairs={{1,0},{2,1},{3,2},{4,3},{5,4},{6,5},{7,6},{8,7},{9,8},{10,9},{11,1... | collective-permute-start | bytes 3145736 | tf_op jit(solution)/shard_map/ppermute | solution.py:459
  9.4 1.2 fusion.1.q
  10.6 0.0 copy-done.9
  10.6 0.2 jit_solution_.3.shift
  10.7 0.0 copy-done.1
  10.8 0.0 copy-done.3
  10.8 0.0 copy-done.4
  10.8 0.0 copy-done.6
  10.8 28.4 %local.1 = (f32[1025,8,128]{2,1,0:T(8,128)S(1)}, bf16[1025,32,128]{2,1,0:T(8,128)(2,1)S(1)}, bf16[1025,16,128]{2,1,0:T(8,128)(2,1)S(1)}, bf16[1025,16,128]{2,1,0...) custom-call(f32[3,512,256]{2,1,0:T(8,128)S(1)} %copy-done.1, f32[512,256]{1,0:T(8,128)S(1)} %fusion.1.q, ...), custom_call_target="tpu_custom_call" | custom-call | tf_op jit(solution)/shard_map/local/pallas_call | solution.py:410
  39.2 0.0 collective-permute-done.rpos
  39.2 0.1 select_reduce_fusion.rcounts
  39.3 38.6 %remote.1 = (f32[1025,8,128]{2,1,0:T(8,128)S(1)}, f32[4,256,256]{2,1,0:T(8,128)S(1)}) custom-call(f32[4,256,256]{2,1,0:T(8,128)S(1)} %collective-permute-done.rpos, s32[512]{0:T(512)S(1)} %copy-done.6, s32[256]{0:T(256)S(1)} %select_reduce_fusion.rcounts, s32[3,896]{1,0:T(4,128)S(1)} %copy-done.4, ...), custom_call_target="tpu_custom_call", output_to_operand_aliasing={{0}: (8, {})} | custom-call | tf_op jit(solution)/shard_map/remote/pallas_call | solution.py:427
  77.9 7.2 %collective-permute-start.1 = (f32[4,256,256]{2,1,0:T(8,128)S(1)}, f32[4,256,256]{2,1,0:T(8,128)S(1)}, u32[]{:S(2)}, u32[]{:S(2)}) collective-permute-start(f32[4,256,256]{2,1,0:T(8,128)S(1)} %get-tuple-element.22), channel_id=1, source_target_pairs={{0,1},{1,2},{2,3},{3,4},{4,5},{5,6},{6,7},{7,8},{8,9},{9,10},{10,1... | collective-permute-start | bytes 3145736 | tf_op jit(solution)/shard_map/ppermute | solution.py:459
  85.1 0.1 fusion.occupied
  85.2 0.0 copy-start.8
  85.2 43.4 %own.1.acc = f32[1025,8,128]{2,1,0:T(8,128)S(1)} custom-call(s32[1168]{0:T(1024)S(1)} %get-tuple-element.14.own, s32[656]{0:T(1024)S(1)} %get-tuple-element.15.half, s32[2]{0:T(128)S(1)} %get-tuple-element.16.sizes, bf16[27,32,128]{2,1,0:T(8,128)(2,1)S(1)} %copy-done.3, ...), custom_call_target="tpu_custom_call", output_to_operand_aliasing={{}: (7, {})} | custom-call | tf_op jit(solution)/shard_map/own/pallas_call | solution.py:439
  128.7 0.0 collective-permute-done.1.back
  128.7 0.0 copy-done.8
  128.7 6.6 %final.1 = f32[4,512,256]{2,1,0:T(8,128)} custom-call(f32[1025,8,128]{2,1,0:T(8,128)S(1)} %own.1.acc, f32[3,512,256]{2,1,0:T(8,128)S(1)} %copy-done.1, f32[512,256]{1,0:T(8,128)S(1)} %fusion.1.q, f32[512,256]{1,0:T(8,128)S(1)} %fusion.occupied, s32[256]{0:T(256)S(1)} %copy-done.8, f32[4,256,256]{2,1,0:T(8,128)S(1)} %collective-permute-done.1.back), custom_call_target="tpu_custom_call" | custom-call | tf_op jit(solution)/shard_map/final/pallas_call | solution.py:450
Async XLA Ops:
  0.0 1.4 %copy-start = (f32[3,512,256]{2,1,0:T(8,128)S(1)}, f32[3,512,256]{2,1,0:T(8,128)}, u32[]{:S(2)}) copy-start(f32[3,512,256]{2,1,0:T(8,128)} %pos.5) | copy-start | bytes 4718596
  1.4 1.0 copy-start.2
  2.5 0.7 copy-start.5
  3.1 0.7 copy-start.7
  3.8 6.7 %copy-start.9 = (f32[27,32]{1,0:T(8,128)S(1)}, f32[27,32]{1,0:T(8,128)}, u32[]{:S(2)}) copy-start(f32[27,32]{1,0:T(8,128)} %constant.25.clone) | copy-start | bytes 10372
  3.8 6.9 %copy-start.1 = (f32[3,512,256]{2,1,0:T(8,128)S(1)}, f32[3,512,256]{2,1,0:T(8,128)}, u32[]{:S(2)}) copy-start(f32[3,512,256]{2,1,0:T(8,128)} %pos.5) | copy-start | bytes 4718596
  3.8 6.9 %copy-start.3 = (bf16[27,32,128]{2,1,0:T(8,128)(2,1)S(1)}, bf16[27,32,128]{2,1,0:T(8,128)(2,1)}, u32[]{:S(2)}) copy-start(bf16[27,32,128]{2,1,0:T(8,128)(2,1)} %constant.24.clone.table) | copy-start | bytes 663556
  3.8 6.9 %copy-start.4 = (s32[3,896]{1,0:T(4,128)S(1)}, s32[3,896]{1,0:T(4,128)}, u32[]{:S(2)}) copy-start(s32[3,896]{1,0:T(4,128)} %pairs.3) | copy-start | bytes 32260
  3.8 7.0 %copy-start.6 = (s32[512]{0:T(512)S(1)}, s32[512]{0:T(512)}, u32[]{:S(2)}) copy-start(s32[512]{0:T(512)} %counts.5) | copy-start | bytes 6148
  6.8 32.4 %collective-permute-start = (f32[4,256,256]{2,1,0:T(8,128)}, f32[4,256,256]{2,1,0:T(8,128)S(1)}, u32[]{:S(2)}, u32[]{:S(2)}) collective-permute-start(f32[4,256,256]{2,1,0:T(8,128)} %gather.1), channel_id=1, source_target_pairs={{1,0},{2,1},{3,2},{4,3},{5,4},{6,5},{7,6},{8,7},{9,8},{10,9},{11,1... | collective-permute-start | bytes 3145736 | tf_op jit(solution)/shard_map/ppermute | solution.py:459
  77.9 50.8 %collective-permute-start.1 = (f32[4,256,256]{2,1,0:T(8,128)S(1)}, f32[4,256,256]{2,1,0:T(8,128)S(1)}, u32[]{:S(2)}, u32[]{:S(2)}) collective-permute-start(f32[4,256,256]{2,1,0:T(8,128)S(1)} %get-tuple-element.22), channel_id=1, source_target_pairs={{0,1},{1,2},{2,3},{3,4},{4,5},{5,6},{6,7},{7,8},{8,9},{9,10},{10,1... | collective-permute-start | bytes 3145736 | tf_op jit(solution)/shard_map/ppermute | solution.py:459
  85.2 43.4 %copy-start.8 = (s32[256]{0:T(256)S(1)}, s32[256]{0:T(256)}, u32[]{:S(2)}) copy-start(s32[256]{0:T(256)} %send.3) | copy-start | bytes 3076
